TPU v7x, 32 devices: a whole 2x2x4 slice. The times are simulated.
32 devices in a mesh: front: 4 (over y, core), row: 4 (over z), col: 2 (over x).
Axes of the slice: x: 2, y: 2, z: 4, core: 2. Of those that a mesh axis runs over, the one named last changes fastest.
Arguments:
- front_matrix: float32 [4, 8192, 8192], P('front', 'row', 'col'), may hold values from -16 to 9216
- child_blocks: bfloat16 [4, 2, 6144, 6144], P('front', None, 'row', 'col'), may hold values from -6 to 6
- child_maps: int32 [4, 2, 48], replicated, may hold values from 0 to 63, as said below
- pivot_rows: int32 [4, 16], replicated, may hold values from 0 to 15, as said below
Outputs:
- factored: float32 [4, 8192, 8192], P('front', 'row', 'col')
Inputs may be any that keep to these rules, and one draw needn't show every extreme that they name: Each row of pivot_rows is a permutation of 0 to 15. Within each child the entries increase, and entry b lies in the same one of 4 equal segments as b: child_maps[f, s, b] div (16) = b div (12).
All inputs are finite; a program needn't handle non-finite values.
Results may differ from a plain program's by a relative error of at most 0.0027.
Values may be sent and summed in bfloat16 or wider, within the bound.
No kernel may reach another device: no remote copies, remote signals or barrier semaphores. Data moves between devices by JAX's collectives and lax.ppermute only.
A program may use at most 256 MiB of HBM per device.

v0:
```python
import jax
import jax.numpy as jnp
from jax import lax
from jax.sharding import PartitionSpec as P

W = 512
NP = 2
MB = 128


def from_partner(block, axis, apart):
    count = lax.axis_size(axis)
    route = []
    for low in range(count):
        high = low | 1 << apart
        if high != low and high < count:
            route += [(low, high), (high, low)]
    return lax.ppermute(block, axis, route)


def spread_2(block, axis, source):
    block = jnp.where(lax.axis_index(axis) == source, block, jnp.zeros_like(block))
    return lax.psum(block, axis)


def extend(piece, block_map, row_id, col_id, map_rows, map_cols):
    child_rows, child_cols = piece.shape
    child_row_blocks = child_rows // MB
    child_col_blocks = child_cols // MB
    row_map = (
        lax.dynamic_slice_in_dim(block_map, row_id * child_row_blocks, child_row_blocks)
        - row_id * map_rows
    )
    col_map = (
        lax.dynamic_slice_in_dim(block_map, col_id * child_col_blocks, child_col_blocks)
        - col_id * map_cols
    )
    row_onehot = (row_map[None, :] == jnp.arange(map_rows)[:, None]).astype(jnp.float32)
    col_onehot = (col_map[None, :] == jnp.arange(map_cols)[:, None]).astype(jnp.float32)
    blocks = piece.astype(jnp.float32).reshape(child_row_blocks, MB, child_col_blocks, MB)
    spread = jnp.einsum("pb,bxcy->pxcy", row_onehot, blocks, precision=lax.Precision.HIGHEST)
    spread = jnp.einsum("pxcy,qc->pxqy", spread, col_onehot, precision=lax.Precision.HIGHEST)
    return spread.reshape(map_rows * MB, map_cols * MB)


def refine(block, is_owner):
    reciprocal = 1.0 / jnp.where(is_owner, jnp.diagonal(block), 1.0)
    first_guess = 2.0 * jnp.diag(reciprocal) - reciprocal[:, None] * block * reciprocal[None, :]
    product = jnp.dot(block, first_guess, precision=lax.Precision.HIGHEST)
    return 2.0 * first_guess - jnp.dot(first_guess, product, precision=lax.Precision.HIGHEST)


def body(front_matrix, child_blocks, child_maps, pivot_rows):
    col_count = lax.axis_size("col")
    row_id = lax.axis_index("row")
    col_id = lax.axis_index("col")
    front_id = lax.axis_index("front")
    matrix = front_matrix[0]
    local_rows, local_cols = matrix.shape
    row_blocks = local_rows // W
    map_rows = local_rows // MB
    map_cols = local_cols // MB
    partner = from_partner(child_blocks[0, 1], "front", 0)
    own_map = lax.dynamic_index_in_dim(child_maps, front_id, 0, keepdims=False)[0]
    partner_map = lax.dynamic_index_in_dim(
        child_maps, jnp.bitwise_xor(front_id, 1), 0, keepdims=False
    )[1]
    matrix = matrix + extend(child_blocks[0, 0], own_map, row_id, col_id, map_rows, map_cols)
    matrix = matrix + extend(partner, partner_map, row_id, col_id, map_rows, map_cols)
    panel_order = lax.dynamic_index_in_dim(pivot_rows, front_id, 0, keepdims=False)
    block_ids = row_id * row_blocks + jnp.arange(row_blocks, dtype=jnp.int32)
    slab_ids = jnp.arange(local_cols // W, dtype=jnp.int32)
    zero_half = jnp.zeros((), jnp.bfloat16)
    pending = None
    for panel in range(NP):
        pivot_index = panel_order[panel]
        owner_row = pivot_index // row_blocks
        row_start = pivot_index % row_blocks * W
        owner_col = panel % col_count
        col_start = panel // col_count * W
        is_owner = col_id == owner_col
        column = matrix[:, col_start : col_start + W]
        row_local = lax.dynamic_slice_in_dim(matrix, row_start, W, 0)
        received = spread_2(row_local, "row", owner_row)
        upper_values = received.astype(jnp.bfloat16)
        pivot_tile = received[:, col_start : col_start + W]
        inverse = refine(pivot_tile, is_owner)
        done_rows = jnp.repeat(
            jnp.any(block_ids[:, None] == panel_order[None, : panel + 1], axis=1), W
        )
        earlier = jnp.repeat(jnp.any(block_ids[:, None] == panel_order[None, :panel], axis=1), W)
        current = jnp.repeat(block_ids == pivot_index, W)
        lower_local = jnp.dot(
            column.astype(jnp.bfloat16),
            inverse.astype(jnp.bfloat16),
            preferred_element_type=jnp.float32,
        ).astype(jnp.bfloat16)
        lower_local = jnp.where(done_rows[:, None], zero_half, lower_local)
        lower_part = spread_2(lower_local, "col", owner_col)
        done_slabs = jnp.zeros(slab_ids.shape, jnp.bool_)
        for earlier_panel in range(panel + 1):
            done_slabs = done_slabs | (col_id == earlier_panel % col_count) & (
                slab_ids == earlier_panel // col_count
            )
        done_cols = jnp.repeat(done_slabs, W)
        upper_part = jnp.where(done_cols[None, :], zero_half, upper_values)
        matrix = matrix - jnp.dot(lower_part, upper_part, preferred_element_type=jnp.float32)
        pending = None
        new_slab = jnp.where(
            earlier[:, None],
            column,
            jnp.where(
                current[:, None], jnp.tile(inverse, (row_blocks, 1)), lower_part.astype(jnp.float32)
            ),
        )
        final_slab = jnp.where(is_owner, new_slab, matrix[:, col_start : col_start + W])
        matrix = matrix.at[:, col_start : col_start + W].set(final_slab)
    return matrix[None]


def solution(mesh):
    in_specs = (P("front", "row", "col"), P("front", None, "row", "col"), P(), P())
    out_specs = P("front", "row", "col")
    return jax.shard_map(body, mesh=mesh, in_specs=in_specs, out_specs=out_specs, check_vma=False)
```

profile of v0, /device:TPU:0, one launch (start us, length us, event | category | flops | bytes accessed | tf_op | source)
XLA Modules:
  0.0 1085.3 jit_solution(17954044593018340265)
XLA Ops:
  6.5 0.0 copy-start
  6.5 0.0 copy-start.7
  6.5 0.0 all-reduce.5.cloned.1.call-start
  6.5 14.5 %slice_bitcast_fusion.1 = (bf16[192,8,24,128]{3,1,2,0:T(8,128)(2,1)}, bf16[1536,3072]{1,0:T(8,128)(2,1)}) fusion(bf16[1,2,1536,3072]{3,2,1,0:T(8,128)(2,1)} %param.9), kind=kLoop, calls=%fused_computation.15 | loop fusion | bytes 37748736
  21.0 0.5 collective-permute-start
  21.5 0.0 copy-done
  21.5 0.0 copy-start.5
  21.5 0.6 copy-done.5
  22.0 0.6 fusion.78
  25.2 0.0 copy-done.7
  25.2 9.8 copy.15
  35.0 0.1 fusion.59
  35.1 0.1 fusion.57
  35.2 18.6 %fusion.6 = f32[16,128,24,128]{3,0,2,1:T(8,128)} fusion(bf16[12,128,24,128]{3,2,1,0:T(8,128)(2,1)} %bitcast.95, s32[12]{0:T(128)S(1)} %get-tuple-element.37), kind=kOutput, calls=%fused_computation.12 | convolution fusion | flops 150995136 | bytes 34603056 | tf_op jit(solution)/shard_map/pb,bxcy->pxcy/dot_general | solution.py:41
  53.7 27.1 %fusion.2 = f32[32,16,128,128]{3,0,2,1:T(8,128)} fusion(f32[16,128,24,128]{3,0,2,1:T(8,128)} %fusion.6, s32[24]{0:T(128)S(1)} %get-tuple-element.39), kind=kOutput, calls=%fused_computation.6 | convolution fusion | flops 2415919872 | bytes 58720352 | tf_op jit(solution)/shard_map/pxcy,qc->pxqy/dot_general | solution.py:42
  80.8 0.0 collective-permute-done
  80.8 9.9 copy.17
  90.7 17.9 %fusion.4 = f32[16,128,24,128]{3,0,2,1:T(8,128)} fusion(bf16[12,128,24,128]{3,2,1,0:T(8,128)(2,1)} %bitcast.96, s32[12]{0:T(128)S(1)} %get-tuple-element.38), kind=kOutput, calls=%fused_computation.10 | convolution fusion | flops 150995136 | bytes 34603056 | tf_op jit(solution)/shard_map/pb,bxcy->pxcy/dot_general | solution.py:41
  108.7 37.6 %fusion = f32[32,16,128,128]{3,0,2,1:T(8,128)} fusion(f32[16,128,24,128]{3,0,2,1:T(8,128)} %fusion.4, s32[24]{0:T(128)S(1)} %get-tuple-element.40), kind=kOutput, calls=%fused_computation.4 | convolution fusion | flops 2415919872 | bytes 58720352 | tf_op jit(solution)/shard_map/pxcy,qc->pxqy/dot_general | solution.py:42
  146.2 77.7 %bitcast_add_fusion = f32[2048,4096]{1,0:T(8,128)} fusion(f32[256,8,32,128]{3,2,1,0:T(8,128)} %bitcast.94, f32[256,8,32,128]{3,2,1,0:T(8,128)} %bitcast.93, f32[1,2048,4096]{2,1,0:T(8,128)} %param.8), kind=kLoop, calls=%fused_computation.2 | loop fusion | flops 16777216 | bytes 134217728 | tf_op jit(solution)/shard_map/add | solution.py:69
  223.9 7.8 dynamic-slice_select_fusion.1
  231.8 0.0 all-reduce.5.cloned.1.call-update
  231.8 0.0 all-reduce.7.cloned.1.call-start
  231.9 0.6 broadcast_compare_fusion.1
  232.5 0.1 broadcast_bitcast_fusion.4
  232.6 292.6 %all-reduce.5.cloned.1.call-done = f32[512,4096]{1,0:T(8,128)} async-done(((f32[512,4096]{1,0:T(8,128)}), f32[512,4096]{1,0:T(8,128)}) %all-reduce.5.cloned.1.call-update) | async-done | bytes 8388624 | tf_op jit(solution)/shard_map/psum | solution.py:23
  525.2 1.3 slice.99
  526.5 4.7 gather_fusion
  531.2 3.6 fusion.25
  534.8 3.6 convolution_subtract_fusion.3
  538.5 4.8 fusion.18
  543.3 0.0 all-reduce.7.cloned.1.call-update
  543.3 0.0 all-reduce.9.cloned.1.call-start
  545.9 0.1 broadcast_bitcast_fusion.1
  546.0 0.7 compare_reduce_fusion.1
  546.7 58.7 %all-reduce.7.cloned.1.call-done = bf16[2048,512]{1,0:T(8,128)(2,1)} async-done(((bf16[2048,512]{1,0:T(8,128)(2,1)}), bf16[2048,512]{1,0:T(8,128)(2,1)}) %all-reduce.7.cloned.1.call-update) | async-done | bytes 2097168 | tf_op jit(solution)/shard_map/psum | solution.py:23
  605.4 0.0 copy-start.3
  605.4 29.6 %convolution_subtract_fusion.1 = f32[2048,4096]{1,0:T(8,128)} fusion(f32[2048,4096]{1,0:T(8,128)} %bitcast_add_fusion, bf16[2048,512]{1,0:T(8,128)(2,1)} %all-reduce.7.cloned.1.call-done, f32[512,4096]{1,0:T(8,128)} %all-reduce.5.cloned.1.call-done, pred[4096]{0:T(1024)(128)(4,1)S(1)} %bitcast.100), kind=kOutput, calls=%fused_computation.9 | convolution fusion | flops 8602517504 | bytes 77598720 | tf_op jit(solution)/shard_map/dot_general | solution.py:107
  635.0 0.0 copy-done.3
  635.0 6.0 constant_dynamic-update-slice_fusion
  641.0 7.7 dynamic-slice_select_fusion
  648.7 0.0 copy-start.6
  648.7 0.0 all-reduce.9.cloned.1.call-update
  648.7 0.0 all-reduce.11.cloned.1.call-start
  648.7 0.6 copy-done.6
  649.3 0.2 compare_reduce_fusion
  649.5 0.1 broadcast_bitcast_fusion.3
  649.6 290.1 %all-reduce.9.cloned.1.call-done = f32[512,4096]{1,0:T(8,128)} async-done(((f32[512,4096]{1,0:T(8,128)}), f32[512,4096]{1,0:T(8,128)}) %all-reduce.9.cloned.1.call-update) | async-done | bytes 8388624 | tf_op jit(solution)/shard_map/psum | solution.py:23
  939.7 1.3 slice.101
  941.0 4.8 gather_fusion.1
  945.8 3.6 fusion.24
  949.4 3.6 convolution_subtract_fusion.2
  953.0 4.8 fusion.20
  957.8 0.0 all-reduce.11.cloned.1.call-update
  957.8 0.6 broadcast_compare_fusion
  958.5 0.1 broadcast_bitcast_fusion.2
  958.6 0.1 broadcast_bitcast_fusion
  958.6 61.3 %all-reduce.11.cloned.1.call-done = bf16[2048,512]{1,0:T(8,128)(2,1)} async-done(((bf16[2048,512]{1,0:T(8,128)(2,1)}), bf16[2048,512]{1,0:T(8,128)(2,1)}) %all-reduce.11.cloned.1.call-update) | async-done | bytes 2097168 | tf_op jit(solution)/shard_map/psum | solution.py:23
  1019.9 29.3 %convolution_subtract_fusion = f32[2048,4096]{1,0:T(8,128)} fusion(f32[2048,4096]{1,0:T(8,128)} %get-tuple-element.35, bf16[2048,512]{1,0:T(8,128)(2,1)} %all-reduce.11.cloned.1.call-done, f32[512,4096]{1,0:T(8,128)} %all-reduce.9.cloned.1.call-done, pred[4096]{0:T(1024)(128)(4,1)S(1)} %bitcast.101), kind=kOutput, calls=%fused_computation.8 | convolution fusion | flops 8602517504 | bytes 77598720 | tf_op jit(solution)/shard_map/dot_general | solution.py:107
  1049.2 24.3 %copy.39 = f32[1,2048,4096]{2,1,0:T(8,128)} copy(f32[1,2048,4096]{2,1,0:T(8,128)} %bitcast.90) | data formatting | bytes 67108864
  1073.5 0.0 copy-done.2
  1073.5 0.0 copy-done.4
  1073.5 4.8 fusion.9
  1078.3 0.0 copy-done.1
  (19 shorter events, 0.1 us)
Async XLA Ops:
  6.5 14.9 %copy-start = (s32[4,16]{1,0:T(4,128)S(1)}, s32[4,16]{1,0:T(4,128)}, u32[]{:S(2)}) copy-start(s32[4,16]{1,0:T(4,128)} %param.11) | copy-start | bytes 772
  6.5 18.7 %copy-start.7 = (s32[4,2,48]{2,1,0:T(2,128)S(1)}, s32[4,2,48]{2,1,0:T(2,128)}, u32[]{:S(2)}) copy-start(s32[4,2,48]{2,1,0:T(2,128)} %param.10) | copy-start | bytes 4612
  6.5 518.6 %all-reduce.5.cloned.1.call-start = ((), (), s32[]{:S(2)}) async-start(), calls=%async_computation | async-start | bytes 16777216 | tf_op jit(solution)/shard_map/psum | solution.py:23
  21.0 59.8 %collective-permute-start = (bf16[1536,3072]{1,0:T(8,128)(2,1)}, bf16[1536,3072]{1,0:T(8,128)(2,1)}, u32[]{:S(2)}, u32[]{:S(2)}) collective-permute-start(bf16[1536,3072]{1,0:T(8,128)(2,1)} %get-tuple-element.30), channel_id=1, source_target_pairs={{0,8},{8,0},{16,24},{24,16},{1,9},{9,1},{17,25},{25,17},{2,10},{10... | collective-permute-start | bytes 28311560 | tf_op jit(solution)/shard_map/ppermute | solution.py:18
  21.5 0.6 copy-start.5
  231.8 373.6 %all-reduce.7.cloned.1.call-start = ((), (), s32[]{:S(2)}) async-start(), calls=%async_computation.1 | async-start | bytes 4194304 | tf_op jit(solution)/shard_map/psum | solution.py:23
  543.3 396.4 %all-reduce.9.cloned.1.call-start = ((), (), s32[]{:S(2)}) async-start(), calls=%async_computation.2 | async-start | bytes 16777216 | tf_op jit(solution)/shard_map/psum | solution.py:23
  605.4 29.6 %copy-start.3 = (bf16[2048,512]{1,0:T(8,128)(2,1)S(1)}, bf16[2048,512]{1,0:T(8,128)(2,1)}, u32[]{:S(2)}) copy-start(bf16[2048,512]{1,0:T(8,128)(2,1)} %all-reduce.7.cloned.1.call-done) | copy-start | bytes 6291460
  648.7 0.7 copy-start.6
  648.7 371.2 %all-reduce.11.cloned.1.call-start = ((), (), s32[]{:S(2)}) async-start(), calls=%async_computation.3 | async-start | bytes 4194304 | tf_op jit(solution)/shard_map/psum | solution.py:23
  1049.2 24.3 %copy-start.2 = (f32[2048,512]{1,0:T(8,128)S(1)}, f32[2048,512]{1,0:T(8,128)}, u32[]{:S(2)}) copy-start(f32[2048,512]{1,0:T(8,128)} %get-tuple-element.36) | copy-start | bytes 12582916
  1049.2 24.3 %copy-start.4 = (bf16[2048,512]{1,0:T(8,128)(2,1)S(1)}, bf16[2048,512]{1,0:T(8,128)(2,1)}, u32[]{:S(2)}) copy-start(bf16[2048,512]{1,0:T(8,128)(2,1)} %all-reduce.11.cloned.1.call-done) | copy-start | bytes 6291460
  1049.2 29.1 %copy-start.1 = (s32[4,16]{1,0:T(4,128)S(1)}, s32[4,16]{1,0:T(4,128)}, u32[]{:S(2)}) copy-start(s32[4,16]{1,0:T(4,128)} %param.11) | copy-start | bytes 772
Sparse Core Ops, SparseCore 0:
  231.9 293.2 all-reduce.4
  543.4 61.9 all-reduce.6
  648.8 290.8 all-reduce.8
  957.9 61.9 all-reduce.10
where the time goes:
time: 1090 us
  waiting for transfers between devices  703 us (64%)
  matrix products  184 us (17%)
  other arithmetic  106 us (10%)
  local copies, waits for them, and re-layouts  72.8 us (7%)
  between operations  18.9 us (2%)
    psum x4, waiting for transfers between devices, spread_2(): return lax.psum(block, axis)  703 us
    add x1, other arithmetic, body(): matrix + extend(partner, partner_map, row_id, col_id, map_rows, map_cols)  77.7 us
    dot_general x2, matrix products, extend(): jnp.einsum('pxcy,qc->pxqy', spread, col_onehot, precision=lax.Precision.H...  64.7 us
    unnamed x30, local copies, waits for them, and re-layouts  60 us
    dot_general x2, matrix products, body(): jnp.dot(lower_part, upper_part, preferred_element_type=jnp.float32)  58.9 us
    dot_general x2, matrix products, extend(): jnp.einsum('pb,bxcy->pxcy', row_onehot, blocks, precision=lax.Precision.H...  36.5 us
  transfers between devices with their start and end apart: 5, of which 4 were waited for; matrix products, arithmetic and copies ran while one was open for 5% of the time, Pallas kernels for 0%

commit v1 on v0

v1 whole, which is shorter than its diff:
```python
import functools

import jax
import jax.numpy as jnp
from jax import lax
from jax.experimental import pallas as pl
from jax.experimental.pallas import tpu as pltpu
from jax.sharding import PartitionSpec as P

W = 512
MB = 128
CH = 256
PB = W // MB
TILE_CHUNKS = W // CH
HBM = pl.BlockSpec(memory_space=pltpu.HBM)
SMEM = pl.BlockSpec(memory_space=pltpu.SMEM)
F32 = jnp.float32
BF16 = jnp.bfloat16
MIB = 1 << 20
VMEM_MIB = 48
VMEM = pl.BlockSpec(memory_space=pltpu.VMEM)

OWNS, DIST, LOCAL, OWN_AT, GOT_AT, SEND_AT, COL, LISTS = 0, 2, 4, 6, 8, 10, 12, 16


class Sizes:
    def __init__(self, rows, cols, front, child):
        self.rows, self.cols = rows, cols
        self.local_rows, self.local_cols = front
        self.child_rows, self.child_cols = child
        self.row_blocks = self.local_rows // W
        self.chunks = self.local_cols // CH
        self.map_rows, self.map_cols = self.local_rows // MB, self.local_cols // MB
        self.own_row = LISTS
        self.got_row = self.own_row + self.map_rows
        self.own_col = self.got_row + self.map_rows
        self.got_col = self.own_col + self.map_cols
        self.plan = self.got_col + self.map_cols


def params(mib):
    return pltpu.CompilerParams(vmem_limit_bytes=mib * MIB)


def make_plan(sz, ids, child_maps, pivot_rows):
    child_row_blocks = sz.child_rows // MB
    child_col_blocks = sz.child_cols // MB

    def place(z):
        return jnp.where(z % 2 == 1, (z + 1) // 2, jnp.where(z == 0, 0, sz.rows - z // 2))

    def kernel(ids_ref, maps_ref, order_ref, out_ref):
        front, row, col = ids_ref[0], ids_ref[1], ids_ref[2]
        partner = jnp.bitwise_xor(front, 1)
        for i in range(COL + 1, LISTS):
            out_ref[i] = 0
        out_ref[COL] = col

        def start(f, s, local):
            count = jnp.int32(0)
            for b in range(child_row_blocks):
                at = maps_ref[f, s, row * child_row_blocks + b] - row * sz.map_rows
                count += (at < local * PB).astype(jnp.int32)
            return jnp.minimum(count, child_row_blocks - PB)

        for p in range(2):
            pivot = order_ref[front, p]
            owner = pivot // sz.row_blocks
            local = pivot - owner * sz.row_blocks
            other = order_ref[partner, p] % sz.row_blocks
            out_ref[OWNS + p] = (owner == row).astype(jnp.int32)
            out_ref[DIST + p] = (place(row) - place(owner) + sz.rows) % sz.rows
            out_ref[LOCAL + p] = local
            out_ref[OWN_AT + p] = start(front, 0, local)
            out_ref[GOT_AT + p] = start(partner, 1, local)
            out_ref[SEND_AT + p] = start(front, 1, other)
        for f, s, row_list, col_list in (
            (front, 0, sz.own_row, sz.own_col),
            (partner, 1, sz.got_row, sz.got_col),
        ):
            for i in range(sz.map_rows):
                out_ref[row_list + i] = -1
            for i in range(sz.map_cols):
                out_ref[col_list + i] = -1
            for b in range(child_row_blocks):
                at = maps_ref[f, s, row * child_row_blocks + b] - row * sz.map_rows
                out_ref[row_list + at] = b
            for b in range(child_col_blocks):
                at = maps_ref[f, s, col * child_col_blocks + b] - col * sz.map_cols
                out_ref[col_list + at] = b

    return pl.pallas_call(
        kernel,
        out_shape=jax.ShapeDtypeStruct((sz.plan,), jnp.int32),
        in_specs=[SMEM] * 3,
        out_specs=SMEM,
        compiler_params=params(VMEM_MIB),
        name="plan",
    )(ids, child_maps, pivot_rows)


def cut_rows(sz, plan, child_blocks, panel):
    def kernel(plan_ref, child_ref, out_ref, sem):
        at = pl.multiple_of(plan_ref[SEND_AT + panel] * MB, MB)
        copy = pltpu.make_async_copy(child_ref.at[0, 1, pl.ds(at, W)], out_ref, sem)
        copy.start()
        copy.wait()

    return pl.pallas_call(
        kernel,
        out_shape=jax.ShapeDtypeStruct((W, sz.child_cols), BF16),
        in_specs=[SMEM, HBM],
        out_specs=VMEM,
        scratch_shapes=[pltpu.SemaphoreType.DMA],
        compiler_params=params(VMEM_MIB),
        name="cut_rows",
    )(plan, child_blocks)


def cut_cols(sz, child_blocks):
    def kernel(child_ref, out_ref, sem):
        copy = pltpu.make_async_copy(child_ref.at[0, 1, :, pl.ds(0, W)], out_ref, sem)
        copy.start()
        copy.wait()

    return pl.pallas_call(
        kernel,
        out_shape=jax.ShapeDtypeStruct((sz.child_rows, W), BF16),
        in_specs=[HBM],
        out_specs=VMEM,
        scratch_shapes=[pltpu.SemaphoreType.DMA],
        compiler_params=params(VMEM_MIB),
        name="cut_cols",
    )(child_blocks)


def place_of(row, col):
    there = jnp.logical_and(row >= 0, col >= 0).astype(F32)
    row_at = pl.multiple_of(jnp.maximum(row, 0) * MB, MB)
    col_at = pl.multiple_of(jnp.maximum(col, 0) * MB, MB)
    return pl.ds(row_at, MB), pl.ds(col_at, MB), there


def pivot_panel(sz, plan, front_matrix, child_blocks, got_rows, panel):
    group = max(g for g in (1, 2, 4) if sz.chunks % g == 0)
    wide = group * CH

    def kernel(plan_ref, front_ref, child_ref, got_ref, rows_ref, tile_ref, own_ref, sem):
        j = pl.program_id(0)
        own_at, got_at = plan_ref[OWN_AT + panel], plan_ref[GOT_AT + panel]
        local = plan_ref[LOCAL + panel]

        @pl.when(j == 0)
        def _():
            at = pl.multiple_of(own_at * MB, MB)
            copy = pltpu.make_async_copy(child_ref.at[0, 0, pl.ds(at, W)], own_ref, sem)
            copy.start()
            copy.wait()

        def value_of(i, q):
            own_col = plan_ref[sz.own_col + j * (wide // MB) + q]
            got_col = plan_ref[sz.got_col + j * (wide // MB) + q]
            r1, c1, f1 = place_of(plan_ref[sz.own_row + local * PB + i] - own_at, own_col)
            r2, c2, f2 = place_of(plan_ref[sz.got_row + local * PB + i] - got_at, got_col)
            value = front_ref[0, pl.ds(i * MB, MB), pl.ds(q * MB, MB)]
            value += own_ref[r1, c1].astype(F32) * f1
            return value + got_ref[r2, c2].astype(F32) * f2

        for q in range(wide // MB):
            for i in range(PB):
                here = pl.ds(q * MB % CH, MB)
                rows_ref[q * MB // CH, pl.ds(i * MB, MB), here] = value_of(i, q).astype(BF16)

        @pl.when(j < max(W // wide, 1))
        def _():
            for q in range(min(wide, W) // MB):
                for i in range(PB):
                    tile_ref[pl.ds(i * MB, MB), pl.ds(q * MB, MB)] = value_of(i, q)

    last_tile = max(W // wide, 1) - 1
    return pl.pallas_call(
        kernel,
        out_shape=(
            jax.ShapeDtypeStruct((sz.chunks, W, CH), BF16),
            jax.ShapeDtypeStruct((W, W), F32),
        ),
        grid_spec=pltpu.PrefetchScalarGridSpec(
            num_scalar_prefetch=1,
            grid=(sz.chunks // group,),
            in_specs=[
                pl.BlockSpec((1, W, wide), lambda j, plan: (0, plan[LOCAL + panel], j)),
                HBM,
                pl.BlockSpec((W, sz.child_cols), lambda j, plan: (0, 0)),
            ],
            out_specs=[
                pl.BlockSpec((group, W, CH), lambda j, plan: (j, 0, 0)),
                pl.BlockSpec((W, min(wide, W)), lambda j, plan: (0, jnp.minimum(j, last_tile))),
            ],
            scratch_shapes=[pltpu.VMEM((W, sz.child_cols), BF16), pltpu.SemaphoreType.DMA],
        ),
        compiler_params=params(VMEM_MIB),
        cost_estimate=pl.CostEstimate(flops=0, bytes_accessed=20 * MIB, transcendentals=0),
        name="pivot_panel",
    )(plan, front_matrix, child_blocks, got_rows)


def first_columns(sz, plan, front_matrix, child_blocks, got_cols):
    def kernel(plan_ref, front_ref, own_ref, got_ref, out_ref):
        r = pl.program_id(0)
        for i in range(PB):
            own_row = plan_ref[sz.own_row + r * PB + i]
            got_row = plan_ref[sz.got_row + r * PB + i]
            for q in range(PB):
                r1, c1, f1 = place_of(own_row, plan_ref[sz.own_col + q])
                r2, c2, f2 = place_of(got_row, plan_ref[sz.got_col + q])
                here = (pl.ds(i * MB, MB), pl.ds(q * MB, MB))
                value = front_ref[0, here[0], here[1]] + own_ref[r1, c1].astype(F32) * f1
                value += got_ref[r2, c2].astype(F32) * f2
                out_ref[here] = value.astype(BF16)

    return pl.pallas_call(
        kernel,
        out_shape=jax.ShapeDtypeStruct((sz.local_rows, W), BF16),
        grid_spec=pltpu.PrefetchScalarGridSpec(
            num_scalar_prefetch=1,
            grid=(sz.row_blocks,),
            in_specs=[
                pl.BlockSpec((1, W, W), lambda r, plan: (0, r, 0)),
                pl.BlockSpec((None, None, sz.child_rows, W), lambda r, plan: (0, 0, 0, 0)),
                pl.BlockSpec((sz.child_rows, W), lambda r, plan: (0, 0)),
            ],
            out_specs=pl.BlockSpec((W, W), lambda r, plan: (r, 0)),
        ),
        compiler_params=params(VMEM_MIB),
        cost_estimate=pl.CostEstimate(flops=0, bytes_accessed=10 * MIB, transcendentals=0),
        name="first_columns",
    )(plan, front_matrix, child_blocks, got_cols)


def begin(panel_rows):
    def kernel(rows_ref, out_ref, sem):
        copy = pltpu.make_async_copy(rows_ref.at[0], out_ref, sem)
        copy.start()
        copy.wait()

    return pl.pallas_call(
        kernel,
        out_shape=jax.ShapeDtypeStruct(panel_rows.shape[1:], BF16),
        in_specs=[HBM],
        out_specs=VMEM,
        scratch_shapes=[pltpu.SemaphoreType.DMA],
        compiler_params=params(VMEM_MIB),
        name="begin",
    )(panel_rows)


def inject(plan, panel_rows, panel, chunk, received):
    put_in = chunk < panel_rows.shape[0]

    def kernel(plan_ref, rows_ref, received_ref, out_ref, held_ref, sems):
        if put_in:

            @pl.when(plan_ref[OWNS + panel] == 1)
            def _():
                for n, (source, target) in enumerate(
                    ((rows_ref.at[chunk], held_ref), (held_ref, out_ref))
                ):
                    copy = pltpu.make_async_copy(source, target, sems.at[n])
                    copy.start()
                    copy.wait()

    return pl.pallas_call(
        kernel,
        out_shape=jax.ShapeDtypeStruct(received.shape, BF16),
        in_specs=[SMEM, HBM, HBM],
        out_specs=HBM,
        scratch_shapes=[pltpu.VMEM(received.shape, BF16), pltpu.SemaphoreType.DMA((2,))],
        input_output_aliases={2: 0},
        compiler_params=params(VMEM_MIB),
        name="inject",
    )(plan, panel_rows, received)


def gather_tiles(sz, plan, passed):
    count = len(passed[0])

    def kernel(plan_ref, *refs):
        sources = (refs[:count], refs[count : 2 * count])
        out_ref, sems = refs[2 * count :]
        for p in range(2):
            for d in range(sz.rows):

                @pl.when(plan_ref[DIST + p] == d)
                def _():
                    for t in range(TILE_CHUNKS):
                        pltpu.make_async_copy(
                            sources[p][t + d], out_ref.at[p, t], sems.at[p, t]
                        ).start()

        for p in range(2):
            for t in range(TILE_CHUNKS):
                pltpu.make_async_copy(sources[p][t], out_ref.at[p, t], sems.at[p, t]).wait()

    return pl.pallas_call(
        kernel,
        out_shape=jax.ShapeDtypeStruct((2, TILE_CHUNKS, W, CH), BF16),
        in_specs=[SMEM] + [HBM] * (2 * count),
        out_specs=VMEM,
        scratch_shapes=[pltpu.SemaphoreType.DMA((2, TILE_CHUNKS))],
        compiler_params=params(VMEM_MIB),
        name="gather_tiles",
    )(plan, *passed[0], *passed[1])


def invert(block):
    rows = lax.broadcasted_iota(jnp.int32, (W, W), 0)
    cols = lax.broadcasted_iota(jnp.int32, (W, W), 1)
    on_diagonal = rows == cols
    diagonal = jnp.where(on_diagonal, block, 0.0)
    down = 1.0 / jnp.sum(diagonal, axis=1, keepdims=True)
    across = 1.0 / jnp.sum(diagonal, axis=0, keepdims=True)
    first = jnp.where(on_diagonal, 2.0 * down, 0.0) - down * block * across
    product = jnp.dot(block, first, precision=lax.Precision.HIGHEST, preferred_element_type=F32)
    return 2.0 * first - jnp.dot(
        first, product, precision=lax.Precision.HIGHEST, preferred_element_type=F32
    )


def tile_algebra(sz, plan, tiles_0, tiles_1, exact_0, exact_1):
    def tile(ref, p):
        return jnp.concatenate([ref[p, t] for t in range(TILE_CHUNKS)], axis=1)

    def kernel(plan_ref, t0_ref, t1_ref, e0_ref, e1_ref, x0_ref, x1_ref, h0_ref, h1_ref, l_ref):
        col = plan_ref[COL]
        mine_0 = jnp.logical_and(plan_ref[OWNS] == 1, col == 0)
        mine_1 = jnp.logical_and(plan_ref[OWNS + 1] == 1, col == 1)
        x0 = invert(jnp.where(mine_0, e0_ref[...], tile(t0_ref, 0).astype(F32)))
        x0_ref[...] = x0
        h0_ref[...] = x0.astype(BF16)
        lower = jnp.dot(tile(t0_ref, 1), h0_ref[...], preferred_element_type=F32).astype(BF16)
        l_ref[...] = lower
        block = jnp.where(mine_1, e1_ref[...], tile(t1_ref, 1).astype(F32))
        block -= jnp.dot(lower, tile(t1_ref, 0), preferred_element_type=F32)
        x1 = invert(block)
        x1_ref[...] = x1
        h1_ref[...] = x1.astype(BF16)

    return pl.pallas_call(
        kernel,
        out_shape=[jax.ShapeDtypeStruct((W, W), t) for t in (F32, F32, BF16, BF16, BF16)],
        in_specs=[SMEM] + [VMEM] * 4,
        out_specs=[VMEM] * 5,
        compiler_params=params(VMEM_MIB),
        name="tile_algebra",
    )(plan, tiles_0, tiles_1, exact_0, exact_1)


def is_pivot(plan_ref, panel, r):
    return jnp.logical_and(plan_ref[OWNS + panel] == 1, plan_ref[LOCAL + panel] == r)


def multipliers(sz, plan, cols_0, cols_1, half_0, half_1, tiles_1):
    def kernel(plan_ref, c0_ref, c1_ref, h0_ref, h1_ref, t1_ref, out_ref):
        r = pl.program_id(0)
        keep_0 = 1.0 - is_pivot(plan_ref, 0, r).astype(F32)
        keep_1 = keep_0 * (1.0 - is_pivot(plan_ref, 1, r).astype(F32))
        upper = jnp.concatenate([t1_ref[0, t] for t in range(TILE_CHUNKS)], axis=1)
        lower_0 = jnp.dot(c0_ref[...], h0_ref[...], preferred_element_type=F32) * keep_0
        lower_0 = lower_0.astype(BF16)
        column = c1_ref[...].astype(F32) - jnp.dot(lower_0, upper, preferred_element_type=F32)
        lower_1 = jnp.dot(column.astype(BF16), h1_ref[...], preferred_element_type=F32) * keep_1
        out_ref[:, :W] = lower_0
        out_ref[:, W:] = lower_1.astype(BF16)

    whole = pl.BlockSpec((W, W), lambda r, plan: (0, 0))
    part = pl.BlockSpec((W, W), lambda r, plan: (r, 0))
    return pl.pallas_call(
        kernel,
        out_shape=jax.ShapeDtypeStruct((sz.local_rows, 2 * W), BF16),
        grid_spec=pltpu.PrefetchScalarGridSpec(
            num_scalar_prefetch=1,
            grid=(sz.row_blocks,),
            in_specs=[
                part,
                part,
                whole,
                whole,
                pl.BlockSpec((2, TILE_CHUNKS, W, CH), lambda r, plan: (0, 0, 0, 0)),
            ],
            out_specs=pl.BlockSpec((W, 2 * W), lambda r, plan: (r, 0)),
        ),
        compiler_params=params(VMEM_MIB),
        cost_estimate=pl.CostEstimate(
            flops=6 * sz.local_rows * W * W, bytes_accessed=10 * MIB, transcendentals=0
        ),
        name="multipliers",
    )(plan, cols_0, cols_1, half_0, half_1, tiles_1)


def update(sz, plan, chunk, front_matrix, child_blocks, partner, lower, lower_1, passed, exact, out):
    special = chunk < TILE_CHUNKS
    per = CH // MB
    blocks = sz.row_blocks
    columns = pl.ds(chunk * CH, CH)

    def kernel(plan_ref, front_ref, own_ref, partner_ref, lower_ref, low_ref, *refs):
        sources = (refs[: sz.rows], refs[sz.rows : 2 * sz.rows])
        refs = refs[2 * sz.rows :]
        if special:
            exact_refs, refs = refs[:2], refs[2:]
        out_ref, f_buf, l_buf, c_buf, x_buf, upper, raw, low, o_buf, sems = refs[-10:]
        targets = (upper.at[pl.ds(0, W)], raw)

        for p in range(2):
            for d in range(sz.rows):

                @pl.when(plan_ref[DIST + p] == d)
                def _():
                    pltpu.make_async_copy(sources[p][d], targets[p], sems.at[p]).start()

        head = [pltpu.make_async_copy(sources[p][0], targets[p], sems.at[p]) for p in range(2)]
        head.append(pltpu.make_async_copy(low_ref, low, sems.at[2]))
        head[2].start()
        children = []
        for n, (child, which, at) in enumerate(
            ((own_ref, 0, sz.own_col), (partner_ref, 1, sz.got_col))
        ):
            for q in range(per):
                b = jnp.maximum(plan_ref[at + chunk * per + q], 0)
                b = pl.ds(pl.multiple_of(b * MB, MB), MB)
                children.append(
                    pltpu.make_async_copy(
                        child.at[0, which, :, b], c_buf.at[n, q], sems.at[3 + n * per + q]
                    )
                )
                children[-1].start()
        base = 3 + 2 * per
        if special:
            for p in range(2):
                children.append(
                    pltpu.make_async_copy(
                        exact_refs[p].at[:, columns], x_buf.at[p], sems.at[base + p]
                    )
                )
                children[-1].start()
        base += 2
        loads, stores = [], []
        for r in range(blocks):
            rows = pl.ds(r * W, W)
            loads.append(
                (
                    pltpu.make_async_copy(
                        front_ref.at[0, rows, columns], f_buf.at[rows], sems.at[base + 3 * r]
                    ),
                    pltpu.make_async_copy(
                        lower_ref.at[rows], l_buf.at[rows], sems.at[base + 3 * r + 1]
                    ),
                )
            )
            stores.append(
                pltpu.make_async_copy(
                    o_buf.at[rows], out_ref.at[0, rows, columns], sems.at[base + 3 * r + 2]
                )
            )
            for copy in loads[-1]:
                copy.start()
        for copy in head:
            copy.wait()
        product = jnp.dot(low[...], upper[:W], preferred_element_type=F32)
        upper[W:] = (raw[...].astype(F32) - product).astype(BF16)
        for copy in children:
            copy.wait()
        for r in range(blocks):
            for copy in loads[r]:
                copy.wait()
            product = jnp.dot(l_buf[r * W : (r + 1) * W], upper[...], preferred_element_type=F32)
            for q in range(per):
                here = pl.ds(q * MB, MB)
                own_col = plan_ref[sz.own_col + chunk * per + q]
                got_col = plan_ref[sz.got_col + chunk * per + q]
                for i in range(PB):
                    rows = pl.ds(r * W + i * MB, MB)
                    r1, _, f1 = place_of(plan_ref[sz.own_row + r * PB + i], own_col)
                    r2, _, f2 = place_of(plan_ref[sz.got_row + r * PB + i], got_col)
                    value = f_buf[rows, here] + c_buf[0, q, r1, :].astype(F32) * f1
                    value += c_buf[1, q, r2, :].astype(F32) * f2
                    value -= product[i * MB : (i + 1) * MB, q * MB : (q + 1) * MB]
                    o_buf[rows, here] = value
            if special:
                col = plan_ref[COL]
                first, second = is_pivot(plan_ref, 0, r), is_pivot(plan_ref, 1, r)
                rows = pl.ds(r * W, W)

                @pl.when(jnp.logical_and(col == 0, first))
                def _():
                    o_buf[rows] = x_buf[0]

                @pl.when(jnp.logical_and(col == 0, jnp.logical_not(first)))
                def _():
                    o_buf[rows] = l_buf[rows, columns].astype(F32)

                @pl.when(jnp.logical_and(col == 1, second))
                def _():
                    o_buf[rows] = x_buf[1]

                @pl.when(jnp.logical_and(col == 1, jnp.logical_not(jnp.logical_or(first, second))))
                def _():
                    o_buf[rows] = l_buf[rows, pl.ds(W + chunk * CH, CH)].astype(F32)

            stores[r].start()
        for copy in stores:
            copy.wait()

    operands = [plan, front_matrix, child_blocks, partner, lower, lower_1]
    operands += list(passed[0]) + list(passed[1])
    if special:
        operands += list(exact)
    aliases = {}
    if out is not None:
        aliases = {len(operands): 0}
        operands.append(out)
    return pl.pallas_call(
        kernel,
        out_shape=jax.ShapeDtypeStruct(front_matrix.shape, F32),
        in_specs=[SMEM] + [HBM] * (len(operands) - 1),
        out_specs=HBM,
        scratch_shapes=[
            pltpu.VMEM((sz.local_rows, CH), F32),
            pltpu.VMEM((sz.local_rows, 2 * W), BF16),
            pltpu.VMEM((2, per, sz.child_rows, MB), BF16),
            pltpu.VMEM((2, W, CH), F32),
            pltpu.VMEM((2 * W, CH), BF16),
            pltpu.VMEM((W, CH), BF16),
            pltpu.VMEM((W, W), BF16),
            pltpu.VMEM((sz.local_rows, CH), F32),
            pltpu.SemaphoreType.DMA((5 + 2 * per + 3 * blocks,)),
        ],
        input_output_aliases=aliases,
        compiler_params=params(VMEM_MIB),
        cost_estimate=pl.CostEstimate(
            flops=4 * sz.local_rows * W * CH, bytes_accessed=10 * MIB, transcendentals=0
        ),
        name="update",
    )(*operands)


def tie(value, *after):
    return lax.optimization_barrier((value, *after))[0]


def from_first_two(cols, col, mine):
    if cols == 2:
        other = lax.ppermute(mine, "col", [(0, 1), (1, 0)])
        return jnp.where(col == 0, mine, other), jnp.where(col == 0, other, mine)
    zero = jnp.zeros_like(mine)
    return tuple(lax.psum(jnp.where(col == c, mine, zero), "col") for c in range(2))


def body(rows, cols, front_matrix, child_blocks, child_maps, pivot_rows):
    sz = Sizes(rows, cols, front_matrix.shape[1:], child_blocks.shape[2:])
    front_count = lax.axis_size("front")
    swap = [(f, f ^ 1) for f in range(front_count)]
    order = [0] + list(range(1, rows, 2)) + sorted(range(2, rows, 2), reverse=True)
    ring = [(order[i], order[(i + 1) % rows]) for i in range(rows)]
    col = lax.axis_index("col")
    ids = jnp.stack([lax.axis_index("front"), lax.axis_index("row"), col]).astype(jnp.int32)
    plan = make_plan(sz, ids, child_maps, pivot_rows)

    got_0 = lax.ppermute(cut_rows(sz, plan, child_blocks, 0), "front", swap)
    rows_0, exact_0 = pivot_panel(sz, plan, front_matrix, child_blocks, got_0, 0)
    got_1 = lax.ppermute(cut_rows(sz, plan, tie(child_blocks, got_0), 1), "front", swap)
    rows_1, exact_1 = pivot_panel(sz, plan, front_matrix, child_blocks, got_1, 1)
    panel_rows = (rows_0, rows_1)

    steps = sz.chunks + rows - 2
    turns = 2 * steps
    tiles_turn = min(2 * rows + 1, turns - 1)
    algebra_turn = min(tiles_turn + 7, turns - 1)
    passed = ([], [])
    held = [None, None]
    state = {"chunk": 0, "out": None}
    after = ()
    partner = None

    def next_update():
        t = state["chunk"]
        state["chunk"] = t + 1
        at = [passed[p][t : t + rows] for p in range(2)]
        state["out"] = update(
            sz, plan, t, front_matrix, child_blocks, partner, lower, lower_1, at, exact, state["out"]
        )

    for turn in range(turns):
        s, k = turn // 2, turn % 2
        if s == 0:
            held[k] = begin(tie(panel_rows[k], *after))
        else:
            held[k] = inject(plan, panel_rows[k], k, s, tie(held[k], *after))
        after = ()
        passed[k].append(held[k])
        if turn == 0:
            send = cut_cols(sz, tie(child_blocks, got_1, held[0]))
            got_cols = lax.ppermute(send, "front", swap)
        held[k] = lax.ppermute(held[k], "row", ring)
        if turn == 1:
            mine = first_columns(sz, plan, front_matrix, child_blocks, tie(got_cols, passed[1][0]))
            partner = lax.ppermute(tie(child_blocks, mine), "front", swap)
            cols_0, cols_1 = from_first_two(cols, col, mine)
            after = (mine,)
        if turn == tiles_turn:
            tiles = gather_tiles(sz, plan, [passed[p][: TILE_CHUNKS + rows - 1] for p in range(2)])
            tiles_0, tiles_1 = from_first_two(cols, col, tiles)
            after = (tiles,)
        if turn == algebra_turn:
            *exact, half_0, half_1, lower_1 = tile_algebra(
                sz, plan, tiles_0, tiles_1, exact_0, exact_1
            )
            after = (lower_1,)
        if turn == algebra_turn + 1 or turn == algebra_turn == turns - 1:
            lower = multipliers(sz, plan, cols_0, cols_1, half_0, half_1, tiles_1)
            after = (lower,)
        if turn > algebra_turn + 1 and 2 * (state["chunk"] + rows - 1) + 1 <= turn:
            next_update()
            after = (state["out"],)
    for k in range(2):
        passed[k].append(held[k])
    while state["chunk"] < sz.chunks:
        next_update()
    return state["out"]


def solution(mesh):
    in_specs = (P("front", "row", "col"), P("front", None, "row", "col"), P(), P())
    out_specs = P("front", "row", "col")
    step = functools.partial(body, mesh.shape["row"], mesh.shape["col"])
    return jax.shard_map(step, mesh=mesh, in_specs=in_specs, out_specs=out_specs, check_vma=False)
```

time: 1090 us -> 334 us (0.31)
  waiting for transfers between devices: 703 us -> 68.1 us
  matrix products: 184 us -> 0 us
  Pallas kernels: 0 us -> 178 us
  other arithmetic: 106 us -> 5.58 us
  starting transfers between devices: 0.58 us -> 50.5 us
  local copies, waits for them, and re-layouts: 72.8 us -> 24.6 us
  between operations: 18.9 us -> 1.35 us
    psum x4 -> x0, waiting for transfers between devices: 703 us -> none  [spread_2(): return lax.psum(block, axis)]
    dot_general x12 -> x0, matrix products: 184 us -> none  [the longest x2 64.7 us: extend(): jnp.einsum('pxcy,qc->pxqy', spread, col_onehot, precision=lax.Precision.H...]
    pallas_call x0 -> x62, Pallas kernels: none -> 178 us  [the longest x16 104 us: update(): pl.pallas_call(kernel, out_shape=jax.ShapeDtypeStruct(front_matrix.shape,...]
    add x2 -> x0, other arithmetic: 77.7 us -> none  [the longest x1 77.7 us: body(): matrix + extend(partner, partner_map, row_id, col_id, map_rows, map_cols)]
    ppermute x1 -> x42, waiting for transfers between devices: 0.01 us -> 68.1 us  [the longest x36 62.8 us: body(): held[k] = lax.ppermute(held[k], 'row', ring)]
    ppermute x1 -> x42, starting transfers between devices: 0.45 us -> 50.5 us  [the longest x36 46.1 us: body(): held[k] = lax.ppermute(held[k], 'row', ring)]
    unnamed x30 -> x76, local copies, waits for them, and re-layouts: 60 us -> 24.6 us
  transfers between devices with their start and end apart: 5 -> 42, of which waited for: 4 -> 19; matrix products, arithmetic and copies ran while one was open for 5% -> 2% of each run, Pallas kernels for 0% -> 47%
where the time goes in v1:
time: 334 us; the launch traced here: 328 us
  Pallas kernels  178 us (53%)
  waiting for transfers between devices  68.1 us (20%)
  starting transfers between devices  50.5 us (15%)
  local copies, waits for them, and re-layouts  24.6 us (7%)
  other arithmetic  5.58 us (2%)
    pallas_call x16, Pallas kernels, update(): pl.pallas_call(kernel, out_shape=jax.ShapeDtypeStruct(front_matrix.shape,...  104 us
    ppermute x36, waiting for transfers between devices, body(): held[k] = lax.ppermute(held[k], 'row', ring)  62.8 us
    ppermute x36, starting transfers between devices, body(): held[k] = lax.ppermute(held[k], 'row', ring)  46.1 us
    unnamed x76, local copies, waits for them, and re-layouts  24.6 us
    pallas_call x2, Pallas kernels, pivot_panel(): pl.pallas_call(kernel, out_shape=(jax.ShapeDtypeStruct((sz.chunks, W, CH)...  20.1 us
    pallas_call x34, Pallas kernels, inject(): pl.pallas_call(kernel, out_shape=jax.ShapeDtypeStruct(received.shape, BF1...  19.8 us
    pallas_call x1, Pallas kernels, tile_algebra(): pl.pallas_call(kernel, out_shape=[jax.ShapeDtypeStruct((W, W), t) for t i...  9.8 us
    pallas_call x1, Pallas kernels, multipliers(): pl.pallas_call(kernel, out_shape=jax.ShapeDtypeStruct((sz.local_rows, 2 *...  7.03 us
  transfers between devices with their start and end apart: 42, of which 19 were waited for; matrix products, arithmetic and copies ran while one was open for 2% of the time, Pallas kernels for 47%

profile of v1, /device:TPU:0, one launch (start us, length us, event | category | flops | bytes accessed | tf_op | source)
XLA Modules:
  0.0 328.2 jit_solution(8521195511613790337)
XLA Ops:
  1.4 1.7 plan.1.plan_ref
  3.2 2.4 cut_rows.2
  6.2 5.3 %collective-permute-done.got_ref = bf16[512,3072]{1,0:T(8,128)(2,1)S(1)} collective-permute-done((bf16[512,3072]{1,0:T(8,128)(2,1)S(1)}, bf16[512,3072]{1,0:T(8,128)(2,1)S(1)}, u32[]{:S(2)}, u32[]{:S(2)}) %collective-permute-start) | collective-permute-done | bytes 3145760 | tf_op jit(solution)/shard_map/ppermute | solution.py:569
  11.4 2.4 cut_rows.3
  14.3 10.0 %pivot_panel.2 = (bf16[16,512,256]{2,1,0:T(8,128)(2,1)}, f32[512,512]{1,0:T(8,128)S(1)}) custom-call(s32[112]{0:T(128)S(1)} %plan.1.plan_ref, f32[1,2048,4096]{2,1,0:T(8,128)} %front_ref.37, bf16[1,2,1536,3072]{3,2,1,0:T(8,128)(2,1)} %own_ref.33, bf16[512,3072]{1,0:T(8,128)(2,1)S(1)} %collective-permute-done.got_ref), custom_call_target="tpu_custom_call" | custom-call | bytes 20971520 | tf_op jit(solution)/shard_map/pivot_panel/pallas_call | solution.py:181
  25.4 2.2 copy-done
  27.6 2.6 cut_cols.1
  30.4 10.0 %pivot_panel.3 = (bf16[16,512,256]{2,1,0:T(8,128)(2,1)}, f32[512,512]{1,0:T(8,128)S(1)}) custom-call(s32[112]{0:T(128)S(1)} %plan.1.plan_ref, f32[1,2048,4096]{2,1,0:T(8,128)} %front_ref.37, bf16[1,2,1536,3072]{3,2,1,0:T(8,128)(2,1)} %own_ref.33, bf16[512,3072]{1,0:T(8,128)(2,1)S(1)} %collective-permute-done.1.got_ref), custom_call_target="tpu_custom_call" | custom-call | bytes 20971520 | tf_op jit(solution)/shard_map/pivot_panel/pallas_call | solution.py:181
  41.5 2.2 copy-done.4
  43.7 6.7 %first_columns.1 = bf16[2048,512]{1,0:T(8,128)(2,1)} custom-call(s32[112]{0:T(128)S(1)} %plan.1.plan_ref, f32[1,2048,4096]{2,1,0:T(8,128)} %front_ref.37, bf16[1,2,1536,3072]{3,2,1,0:T(8,128)(2,1)} %own_ref.33, bf16[1536,512]{1,0:T(8,128)(2,1)S(1)} %collective-permute-done.2.got_ref), custom_call_target="tpu_custom_call" | custom-call | bytes 10485760 | tf_op jit(solution)/shard_map/first_columns/pallas_call | solution.py:221
  50.8 2.7 collective-permute-start.9
  53.5 2.6 collective-permute-start.5
  56.1 5.6 %collective-permute-done.9.received_ref = bf16[512,256]{1,0:T(8,128)(2,1)S(1)} collective-permute-done((bf16[512,256]{1,0:T(8,128)(2,1)S(1)}, bf16[512,256]{1,0:T(8,128)(2,1)S(1)}, u32[]{:S(2)}, u32[]{:S(2)}) %collective-permute-start.9) | collective-permute-done | bytes 262176 | tf_op jit(solution)/shard_map/ppermute | solution.py:604
  63.4 3.9 %collective-permute-done.5.received_ref = bf16[512,256]{1,0:T(8,128)(2,1)S(1)} collective-permute-done((bf16[512,256]{1,0:T(8,128)(2,1)S(1)}, bf16[512,256]{1,0:T(8,128)(2,1)S(1)}, u32[]{:S(2)}, u32[]{:S(2)}) %collective-permute-start.5) | collective-permute-done | bytes 262176 | tf_op jit(solution)/shard_map/ppermute | solution.py:604
  70.4 2.5 collective-permute-done.10.received_ref
  74.6 3.9 %collective-permute-done.6.received_ref = bf16[512,256]{1,0:T(8,128)(2,1)S(1)} collective-permute-done((bf16[512,256]{1,0:T(8,128)(2,1)S(1)}, bf16[512,256]{1,0:T(8,128)(2,1)S(1)}, u32[]{:S(2)}, u32[]{:S(2)}) %collective-permute-start.6) | collective-permute-done | bytes 262176 | tf_op jit(solution)/shard_map/ppermute | solution.py:604
  80.2 3.9 %collective-permute-done.11.received_ref = bf16[512,256]{1,0:T(8,128)(2,1)S(1)} collective-permute-done((bf16[512,256]{1,0:T(8,128)(2,1)S(1)}, bf16[512,256]{1,0:T(8,128)(2,1)S(1)}, u32[]{:S(2)}, u32[]{:S(2)}) %collective-permute-start.11) | collective-permute-done | bytes 262176 | tf_op jit(solution)/shard_map/ppermute | solution.py:604
  85.8 3.9 %collective-permute-done.7.received_ref = bf16[512,256]{1,0:T(8,128)(2,1)S(1)} collective-permute-done((bf16[512,256]{1,0:T(8,128)(2,1)S(1)}, bf16[512,256]{1,0:T(8,128)(2,1)S(1)}, u32[]{:S(2)}, u32[]{:S(2)}) %collective-permute-start.7) | collective-permute-done | bytes 262176 | tf_op jit(solution)/shard_map/ppermute | solution.py:604
  91.4 3.9 %collective-permute-done.12.received_ref = bf16[512,256]{1,0:T(8,128)(2,1)S(1)} collective-permute-done((bf16[512,256]{1,0:T(8,128)(2,1)S(1)}, bf16[512,256]{1,0:T(8,128)(2,1)S(1)}, u32[]{:S(2)}, u32[]{:S(2)}) %collective-permute-start.12) | collective-permute-done | bytes 262176 | tf_op jit(solution)/shard_map/ppermute | solution.py:604
  96.0 4.7 %collective-permute-done.8.received_ref = bf16[512,256]{1,0:T(8,128)(2,1)S(1)} collective-permute-done((bf16[512,256]{1,0:T(8,128)(2,1)S(1)}, bf16[512,256]{1,0:T(8,128)(2,1)S(1)}, u32[]{:S(2)}, u32[]{:S(2)}) %collective-permute-start.8) | collective-permute-done | bytes 262176 | tf_op jit(solution)/shard_map/ppermute | solution.py:604
  101.3 1.7 gather_tiles.1
  103.0 1.5 collective-permute-start.13
  105.3 3.4 %collective-permute-start.14 = (bf16[512,256]{1,0:T(8,128)(2,1)S(1)}, bf16[512,256]{1,0:T(8,128)(2,1)S(1)}, u32[]{:S(2)}, u32[]{:S(2)}) collective-permute-start(bf16[512,256]{1,0:T(8,128)(2,1)S(1)} %inject.37.refs_4_.refs_3_.refs_2_.refs_1_.refs_0_), channel_id=1, source_target_pairs={{0,2},{2,6},{6,4},{4,0},{1,3},{3,7},{7,5},{5,1},{8,10},{10,14},{14... | collective-permute-start | bytes 786440 | tf_op jit(solution)/shard_map/ppermute | solution.py:604
  108.7 5.9 %collective-permute-done.21.received_ref = bf16[512,256]{1,0:T(8,128)(2,1)S(1)} collective-permute-done((bf16[512,256]{1,0:T(8,128)(2,1)S(1)}, bf16[512,256]{1,0:T(8,128)(2,1)S(1)}, u32[]{:S(2)}, u32[]{:S(2)}) %collective-permute-start.21) | collective-permute-done | bytes 262176 | tf_op jit(solution)/shard_map/ppermute | solution.py:604
  116.1 4.1 %collective-permute-done.14.received_ref = bf16[512,256]{1,0:T(8,128)(2,1)S(1)} collective-permute-done((bf16[512,256]{1,0:T(8,128)(2,1)S(1)}, bf16[512,256]{1,0:T(8,128)(2,1)S(1)}, u32[]{:S(2)}, u32[]{:S(2)}) %collective-permute-start.14) | collective-permute-done | bytes 262176 | tf_op jit(solution)/shard_map/ppermute | solution.py:604
  121.7 4.2 %collective-permute-done.22.received_ref = bf16[512,256]{1,0:T(8,128)(2,1)S(1)} collective-permute-done((bf16[512,256]{1,0:T(8,128)(2,1)S(1)}, bf16[512,256]{1,0:T(8,128)(2,1)S(1)}, u32[]{:S(2)}, u32[]{:S(2)}) %collective-permute-start.22) | collective-permute-done | bytes 262176 | tf_op jit(solution)/shard_map/ppermute | solution.py:604
  127.3 4.2 %collective-permute-done.15.received_ref = bf16[512,256]{1,0:T(8,128)(2,1)S(1)} collective-permute-done((bf16[512,256]{1,0:T(8,128)(2,1)S(1)}, bf16[512,256]{1,0:T(8,128)(2,1)S(1)}, u32[]{:S(2)}, u32[]{:S(2)}) %collective-permute-start.15) | collective-permute-done | bytes 262176 | tf_op jit(solution)/shard_map/ppermute | solution.py:604
  132.9 4.2 %collective-permute-done.24.received_ref = bf16[512,256]{1,0:T(8,128)(2,1)S(1)} collective-permute-done((bf16[512,256]{1,0:T(8,128)(2,1)S(1)}, bf16[512,256]{1,0:T(8,128)(2,1)S(1)}, u32[]{:S(2)}, u32[]{:S(2)}) %collective-permute-start.24) | collective-permute-done | bytes 262176 | tf_op jit(solution)/shard_map/ppermute | solution.py:604
  137.1 2.2 copy-done.6
  141.8 2.2 copy-done.2
  144.6 2.8 collective-permute-start.17
  147.4 1.7 broadcast_select_fusion.2
  149.1 9.8 %tile_algebra.1 = (f32[512,512]{1,0:T(8,128)S(1)}, f32[512,512]{1,0:T(8,128)S(1)}, bf16[512,512]{1,0:T(8,128)(2,1)S(1)}, bf16[512,512]{1,0:T(8,128)(2,1)S(1)}, bf16[512,512]{1,0:T(8,128)(2,1)S(1)}) custom-call(s32[112]{0:T(128)S(1)} %plan.1.plan_ref, bf16[2,2,512,256]{3,2,1,0:T(8,128)(2,1)S(1)} %get-tuple-element.70.t0_ref, ...), custom_call_target="tpu_custom_call" | custom-call | tf_op jit(solution)/shard_map/tile_algebra/pallas_call | solution.py:348
  161.0 2.2 copy-done.7
  163.8 2.0 collective-permute-start.27
  166.4 3.8 %broadcast_select_fusion = (bf16[2048,512]{1,0:T(8,128)(2,1)}, bf16[2048,512]{1,0:T(8,128)(2,1)S(1)}) fusion(bf16[2048,512]{1,0:T(8,128)(2,1)} %collective-permute-done.4, bf16[2048,512]{1,0:T(8,128)(2,1)} %first_columns.1, pred[]{:T(512)S(6)} %eq.2), kind=kLoop, calls=%fused_computation | loop fusion | flops 2097152 | bytes 8388609 | tf_op jit(solution)/shard_map/jit(_where)/select_n | solution.py:554
  170.2 7.0 %multipliers.1.lower_ref = bf16[2048,1024]{1,0:T(8,128)(2,1)} custom-call(s32[112]{0:T(128)S(1)} %plan.1.plan_ref, bf16[2048,512]{1,0:T(8,128)(2,1)S(1)} %get-tuple-element.68.c0_ref, bf16[2048,512]{1,0:T(8,128)(2,1)} %get-tuple-element.67.c1_ref, bf16[512,512]{1,0:T(8,128)(2,1)S(1)} %get-tuple-element.45.h0_ref, ...), custom_call_target="tpu_custom_call" | custom-call | flops 3221225472 | bytes 10485760 | tf_op jit(solution)/shard_map/multipliers/pallas_call | solution.py:377
  186.8 6.9 %update.16.refs_10_ = f32[1,2048,4096]{2,1,0:T(8,128)} custom-call(s32[112]{0:T(128)S(1)} %plan.1.plan_ref, f32[1,2048,4096]{2,1,0:T(8,128)} %front_ref.37, bf16[1,2,1536,3072]{3,2,1,0:T(8,128)(2,1)} %own_ref.33, bf16[1,2,1536,3072]{3,2,1,0:T(8,128)(2,1)} %collective-permute-done.3.partner_ref, bf16[2048,1024]{1,0:T(8,128)(2,1)} %multipliers.1.lower_ref, ...), custom_call_target="tpu_custom_call" | custom-call | flops 1073741824 | bytes 10485760 | tf_op jit(solution)/shard_map/update/pallas_call | solution.py:522
  194.3 2.4 collective-permute-start.28
  196.7 6.8 %update.17.refs_8_ = f32[1,2048,4096]{2,1,0:T(8,128)} custom-call(s32[112]{0:T(128)S(1)} %plan.1.plan_ref, f32[1,2048,4096]{2,1,0:T(8,128)} %front_ref.37, bf16[1,2,1536,3072]{3,2,1,0:T(8,128)(2,1)} %own_ref.33, bf16[1,2,1536,3072]{3,2,1,0:T(8,128)(2,1)} %collective-permute-done.3.partner_ref, ...), custom_call_target="tpu_custom_call", output_to_operand_aliasing={{}: (16, {})} | custom-call | flops 1073741824 | bytes 10485760 | tf_op jit(solution)/shard_map/update/pallas_call | solution.py:522
  204.0 1.9 collective-permute-start.20
  206.0 6.4 %update.18.refs_8_ = f32[1,2048,4096]{2,1,0:T(8,128)} custom-call(s32[112]{0:T(128)S(1)} %plan.1.plan_ref, f32[1,2048,4096]{2,1,0:T(8,128)} %front_ref.37, bf16[1,2,1536,3072]{3,2,1,0:T(8,128)(2,1)} %own_ref.33, bf16[1,2,1536,3072]{3,2,1,0:T(8,128)(2,1)} %collective-permute-done.3.partner_ref, ...), custom_call_target="tpu_custom_call", output_to_operand_aliasing={{}: (14, {})} | custom-call | flops 1073741824 | bytes 10485760 | tf_op jit(solution)/shard_map/update/pallas_call | solution.py:522
  213.1 6.4 %update.19.refs_8_ = f32[1,2048,4096]{2,1,0:T(8,128)} custom-call(s32[112]{0:T(128)S(1)} %plan.1.plan_ref, f32[1,2048,4096]{2,1,0:T(8,128)} %front_ref.37, bf16[1,2,1536,3072]{3,2,1,0:T(8,128)(2,1)} %own_ref.33, bf16[1,2,1536,3072]{3,2,1,0:T(8,128)(2,1)} %collective-permute-done.3.partner_ref, ...), custom_call_target="tpu_custom_call", output_to_operand_aliasing={{}: (14, {})} | custom-call | flops 1073741824 | bytes 10485760 | tf_op jit(solution)/shard_map/update/pallas_call | solution.py:522
  220.9 6.4 %update.20.refs_8_ = f32[1,2048,4096]{2,1,0:T(8,128)} custom-call(s32[112]{0:T(128)S(1)} %plan.1.plan_ref, f32[1,2048,4096]{2,1,0:T(8,128)} %front_ref.37, bf16[1,2,1536,3072]{3,2,1,0:T(8,128)(2,1)} %own_ref.33, bf16[1,2,1536,3072]{3,2,1,0:T(8,128)(2,1)} %collective-permute-done.3.partner_ref, ...), custom_call_target="tpu_custom_call", output_to_operand_aliasing={{}: (14, {})} | custom-call | flops 1073741824 | bytes 10485760 | tf_op jit(solution)/shard_map/update/pallas_call | solution.py:522
  227.9 2.4 collective-permute-start.31
  230.2 6.4 %update.21.refs_8_ = f32[1,2048,4096]{2,1,0:T(8,128)} custom-call(s32[112]{0:T(128)S(1)} %plan.1.plan_ref, f32[1,2048,4096]{2,1,0:T(8,128)} %front_ref.37, bf16[1,2,1536,3072]{3,2,1,0:T(8,128)(2,1)} %own_ref.33, bf16[1,2,1536,3072]{3,2,1,0:T(8,128)(2,1)} %collective-permute-done.3.partner_ref, ...), custom_call_target="tpu_custom_call", output_to_operand_aliasing={{}: (14, {})} | custom-call | flops 1073741824 | bytes 10485760 | tf_op jit(solution)/shard_map/update/pallas_call | solution.py:522
  237.2 1.9 collective-permute-start.26
  239.1 6.6 %update.22.refs_8_ = f32[1,2048,4096]{2,1,0:T(8,128)} custom-call(s32[112]{0:T(128)S(1)} %plan.1.plan_ref, f32[1,2048,4096]{2,1,0:T(8,128)} %front_ref.37, bf16[1,2,1536,3072]{3,2,1,0:T(8,128)(2,1)} %own_ref.33, bf16[1,2,1536,3072]{3,2,1,0:T(8,128)(2,1)} %collective-permute-done.3.partner_ref, ...), custom_call_target="tpu_custom_call", output_to_operand_aliasing={{}: (14, {})} | custom-call | flops 1073741824 | bytes 10485760 | tf_op jit(solution)/shard_map/update/pallas_call | solution.py:522
  246.5 6.4 %update.23.refs_8_ = f32[1,2048,4096]{2,1,0:T(8,128)} custom-call(s32[112]{0:T(128)S(1)} %plan.1.plan_ref, f32[1,2048,4096]{2,1,0:T(8,128)} %front_ref.37, bf16[1,2,1536,3072]{3,2,1,0:T(8,128)(2,1)} %own_ref.33, bf16[1,2,1536,3072]{3,2,1,0:T(8,128)(2,1)} %collective-permute-done.3.partner_ref, ...), custom_call_target="tpu_custom_call", output_to_operand_aliasing={{}: (14, {})} | custom-call | flops 1073741824 | bytes 10485760 | tf_op jit(solution)/shard_map/update/pallas_call | solution.py:522
  254.2 6.4 %update.24.refs_8_ = f32[1,2048,4096]{2,1,0:T(8,128)} custom-call(s32[112]{0:T(128)S(1)} %plan.1.plan_ref, f32[1,2048,4096]{2,1,0:T(8,128)} %front_ref.37, bf16[1,2,1536,3072]{3,2,1,0:T(8,128)(2,1)} %own_ref.33, bf16[1,2,1536,3072]{3,2,1,0:T(8,128)(2,1)} %collective-permute-done.3.partner_ref, ...), custom_call_target="tpu_custom_call", output_to_operand_aliasing={{}: (14, {})} | custom-call | flops 1073741824 | bytes 10485760 | tf_op jit(solution)/shard_map/update/pallas_call | solution.py:522
  261.2 2.4 collective-permute-start.34
  263.6 6.4 %update.25.refs_8_ = f32[1,2048,4096]{2,1,0:T(8,128)} custom-call(s32[112]{0:T(128)S(1)} %plan.1.plan_ref, f32[1,2048,4096]{2,1,0:T(8,128)} %front_ref.37, bf16[1,2,1536,3072]{3,2,1,0:T(8,128)(2,1)} %own_ref.33, bf16[1,2,1536,3072]{3,2,1,0:T(8,128)(2,1)} %collective-permute-done.3.partner_ref, ...), custom_call_target="tpu_custom_call", output_to_operand_aliasing={{}: (14, {})} | custom-call | flops 1073741824 | bytes 10485760 | tf_op jit(solution)/shard_map/update/pallas_call | solution.py:522
  270.6 1.9 collective-permute-start.32
  272.5 6.4 %update.26.refs_8_ = f32[1,2048,4096]{2,1,0:T(8,128)} custom-call(s32[112]{0:T(128)S(1)} %plan.1.plan_ref, f32[1,2048,4096]{2,1,0:T(8,128)} %front_ref.37, bf16[1,2,1536,3072]{3,2,1,0:T(8,128)(2,1)} %own_ref.33, bf16[1,2,1536,3072]{3,2,1,0:T(8,128)(2,1)} %collective-permute-done.3.partner_ref, ...), custom_call_target="tpu_custom_call", output_to_operand_aliasing={{}: (14, {})} | custom-call | flops 1073741824 | bytes 10485760 | tf_op jit(solution)/shard_map/update/pallas_call | solution.py:522
  279.6 6.6 %update.27.refs_8_ = f32[1,2048,4096]{2,1,0:T(8,128)} custom-call(s32[112]{0:T(128)S(1)} %plan.1.plan_ref, f32[1,2048,4096]{2,1,0:T(8,128)} %front_ref.37, bf16[1,2,1536,3072]{3,2,1,0:T(8,128)(2,1)} %own_ref.33, bf16[1,2,1536,3072]{3,2,1,0:T(8,128)(2,1)} %collective-permute-done.3.partner_ref, ...), custom_call_target="tpu_custom_call", output_to_operand_aliasing={{}: (14, {})} | custom-call | flops 1073741824 | bytes 10485760 | tf_op jit(solution)/shard_map/update/pallas_call | solution.py:522
  287.6 2.0 collective-permute-done.36.received_ref
  290.6 6.4 %update.28.refs_8_ = f32[1,2048,4096]{2,1,0:T(8,128)} custom-call(s32[112]{0:T(128)S(1)} %plan.1.plan_ref, f32[1,2048,4096]{2,1,0:T(8,128)} %front_ref.37, bf16[1,2,1536,3072]{3,2,1,0:T(8,128)(2,1)} %own_ref.33, bf16[1,2,1536,3072]{3,2,1,0:T(8,128)(2,1)} %collective-permute-done.3.partner_ref, ...), custom_call_target="tpu_custom_call", output_to_operand_aliasing={{}: (14, {})} | custom-call | flops 1073741824 | bytes 10485760 | tf_op jit(solution)/shard_map/update/pallas_call | solution.py:522
  297.6 1.9 collective-permute-start.37
  299.5 2.8 collective-permute-done.38.received_ref
  302.9 6.4 %update.29.refs_8_ = f32[1,2048,4096]{2,1,0:T(8,128)} custom-call(s32[112]{0:T(128)S(1)} %plan.1.plan_ref, f32[1,2048,4096]{2,1,0:T(8,128)} %front_ref.37, bf16[1,2,1536,3072]{3,2,1,0:T(8,128)(2,1)} %own_ref.33, bf16[1,2,1536,3072]{3,2,1,0:T(8,128)(2,1)} %collective-permute-done.3.partner_ref, ...), custom_call_target="tpu_custom_call", output_to_operand_aliasing={{}: (14, {})} | custom-call | flops 1073741824 | bytes 10485760 | tf_op jit(solution)/shard_map/update/pallas_call | solution.py:522
  309.9 1.7 collective-permute-start.39
  311.6 1.9 collective-permute-done.40.received_ref
  314.7 6.4 %update.30.refs_8_ = f32[1,2048,4096]{2,1,0:T(8,128)} custom-call(s32[112]{0:T(128)S(1)} %plan.1.plan_ref, f32[1,2048,4096]{2,1,0:T(8,128)} %front_ref.37, bf16[1,2,1536,3072]{3,2,1,0:T(8,128)(2,1)} %own_ref.33, bf16[1,2,1536,3072]{3,2,1,0:T(8,128)(2,1)} %collective-permute-done.3.partner_ref, ...), custom_call_target="tpu_custom_call", output_to_operand_aliasing={{}: (14, {})} | custom-call | flops 1073741824 | bytes 10485760 | tf_op jit(solution)/shard_map/update/pallas_call | solution.py:522
  321.4 6.4 %update.31 = f32[1,2048,4096]{2,1,0:T(8,128)} custom-call(s32[112]{0:T(128)S(1)} %plan.1.plan_ref, f32[1,2048,4096]{2,1,0:T(8,128)} %front_ref.37, bf16[1,2,1536,3072]{3,2,1,0:T(8,128)(2,1)} %own_ref.33, bf16[1,2,1536,3072]{3,2,1,0:T(8,128)(2,1)} %collective-permute-done.3.partner_ref, ...), custom_call_target="tpu_custom_call", output_to_operand_aliasing={{}: (14, {})} | custom-call | flops 1073741824 | bytes 10485760 | tf_op jit(solution)/shard_map/update/pallas_call | solution.py:522
  (161 shorter events, 54.0 us)
Async XLA Ops:
  5.6 5.8 %collective-permute-start = (bf16[512,3072]{1,0:T(8,128)(2,1)S(1)}, bf16[512,3072]{1,0:T(8,128)(2,1)S(1)}, u32[]{:S(2)}, u32[]{:S(2)}) collective-permute-start(bf16[512,3072]{1,0:T(8,128)(2,1)S(1)} %cut_rows.2), channel_id=1, source_target_pairs={{0,8},{8,0},{16,24},{24,16},{1,9},{9,1},{17,25},{25,17},{2,10},{10... | collective-permute-start | bytes 9437192 | tf_op jit(solution)/shard_map/ppermute | solution.py:569
  13.9 13.7 %collective-permute-start.1 = (bf16[512,3072]{1,0:T(8,128)(2,1)S(1)}, bf16[512,3072]{1,0:T(8,128)(2,1)S(1)}, u32[]{:S(2)}, u32[]{:S(2)}) collective-permute-start(bf16[512,3072]{1,0:T(8,128)(2,1)S(1)} %cut_rows.3), channel_id=1, source_target_pairs={{0,8},{8,0},{16,24},{24,16},{1,9},{9,1},{17,25},{25,17},{2,10},{10... | collective-permute-start | bytes 9437192 | tf_op jit(solution)/shard_map/ppermute | solution.py:571
  27.6 73.6 %copy-start.30 = (bf16[512,256]{1,0:T(8,128)(2,1)}, bf16[512,256]{1,0:T(8,128)(2,1)S(1)}, u32[]{:S(2)}) copy-start(bf16[512,256]{1,0:T(8,128)(2,1)S(1)} %begin.2.refs_0_) | copy-start | bytes 786436
  30.3 13.5 %collective-permute-start.2 = (bf16[1536,512]{1,0:T(8,128)(2,1)}, bf16[1536,512]{1,0:T(8,128)(2,1)S(1)}, u32[]{:S(2)}, u32[]{:S(2)}) collective-permute-start(bf16[1536,512]{1,0:T(8,128)(2,1)} %cut_cols.1), channel_id=1, source_target_pairs={{0,8},{8,0},{16,24},{24,16},{1,9},{9,1},{17,25},{25,17},{2,10},{10... | collective-permute-start | bytes 4718600 | tf_op jit(solution)/shard_map/ppermute | solution.py:603
  43.7 57.6 %copy-start.32 = (bf16[512,256]{1,0:T(8,128)(2,1)}, bf16[512,256]{1,0:T(8,128)(2,1)S(1)}, u32[]{:S(2)}) copy-start(bf16[512,256]{1,0:T(8,128)(2,1)S(1)} %begin.3.refs_5_.refs_4_) | copy-start | bytes 786436
  43.7 17.9 %copy-start.5 = (bf16[16,512,256]{2,1,0:T(8,128)(2,1)S(1)}, bf16[16,512,256]{2,1,0:T(8,128)(2,1)}, u32[]{:S(2)}) copy-start(bf16[16,512,256]{2,1,0:T(8,128)(2,1)} %get-tuple-element.39.rows_ref) | copy-start | bytes 12582916
  43.7 23.6 %copy-start.1 = (bf16[16,512,256]{2,1,0:T(8,128)(2,1)S(1)}, bf16[16,512,256]{2,1,0:T(8,128)(2,1)}, u32[]{:S(2)}) copy-start(bf16[16,512,256]{2,1,0:T(8,128)(2,1)} %get-tuple-element.37.rows_ref) | copy-start | bytes 12582916
  50.4 128.2 %collective-permute-start.3 = (bf16[1,2,1536,3072]{3,2,1,0:T(8,128)(2,1)}, bf16[1,2,1536,3072]{3,2,1,0:T(8,128)(2,1)}, u32[]{:S(2)}, u32[]{:S(2)}) collective-permute-start(bf16[1,2,1536,3072]{3,2,1,0:T(8,128)(2,1)} %own_ref.33), channel_id=1, source_target_pairs={{0,8},{8,0},{16,24},{24,16},{1,9},{9,1},{17,25},{25,17},{2,10},{10... | collective-permute-start | bytes 56623112 | tf_op jit(solution)/shard_map/ppermute | solution.py:607
  50.8 10.9 %collective-permute-start.9 = (bf16[512,256]{1,0:T(8,128)(2,1)S(1)}, bf16[512,256]{1,0:T(8,128)(2,1)S(1)}, u32[]{:S(2)}, u32[]{:S(2)}) collective-permute-start(bf16[512,256]{1,0:T(8,128)(2,1)S(1)} %begin.3.refs_5_.refs_4_), channel_id=1, source_target_pairs={{0,2},{2,6},{6,4},{4,0},{1,3},{3,7},{7,5},{5,1},{8,10},{10,14},{14... | collective-permute-start | bytes 786440 | tf_op jit(solution)/shard_map/ppermute | solution.py:604
  53.5 13.8 %collective-permute-start.5 = (bf16[512,256]{1,0:T(8,128)(2,1)S(1)}, bf16[512,256]{1,0:T(8,128)(2,1)S(1)}, u32[]{:S(2)}, u32[]{:S(2)}) collective-permute-start(bf16[512,256]{1,0:T(8,128)(2,1)S(1)} %begin.2.refs_0_), channel_id=1, source_target_pairs={{0,2},{2,6},{6,4},{4,0},{1,3},{3,7},{7,5},{5,1},{8,10},{10,14},{14... | collective-permute-start | bytes 786440 | tf_op jit(solution)/shard_map/ppermute | solution.py:604
  62.3 53.0 %copy-start.28 = (bf16[512,256]{1,0:T(8,128)(2,1)}, bf16[512,256]{1,0:T(8,128)(2,1)S(1)}, u32[]{:S(2)}) copy-start(bf16[512,256]{1,0:T(8,128)(2,1)S(1)} %inject.38.refs_6_.refs_5_.refs_4_) | copy-start | bytes 786436
  62.3 10.6 %collective-permute-start.10 = (bf16[512,256]{1,0:T(8,128)(2,1)S(1)}, bf16[512,256]{1,0:T(8,128)(2,1)S(1)}, u32[]{:S(2)}, u32[]{:S(2)}) collective-permute-start(bf16[512,256]{1,0:T(8,128)(2,1)S(1)} %inject.38.refs_6_.refs_5_.refs_4_), channel_id=1, source_target_pairs={{0,2},{2,6},{6,4},{4,0},{1,3},{3,7},{7,5},{5,1},{8,10},{10,14},{14... | collective-permute-start | bytes 786440 | tf_op jit(solution)/shard_map/ppermute | solution.py:604
  67.8 53.0 %copy-start.26 = (bf16[512,256]{1,0:T(8,128)(2,1)}, bf16[512,256]{1,0:T(8,128)(2,1)S(1)}, u32[]{:S(2)}) copy-start(bf16[512,256]{1,0:T(8,128)(2,1)S(1)} %inject.34.refs_1_.refs_0_) | copy-start | bytes 786436
  67.8 10.6 %collective-permute-start.6 = (bf16[512,256]{1,0:T(8,128)(2,1)S(1)}, bf16[512,256]{1,0:T(8,128)(2,1)S(1)}, u32[]{:S(2)}, u32[]{:S(2)}) collective-permute-start(bf16[512,256]{1,0:T(8,128)(2,1)S(1)} %inject.34.refs_1_.refs_0_), channel_id=1, source_target_pairs={{0,2},{2,6},{6,4},{4,0},{1,3},{3,7},{7,5},{5,1},{8,10},{10,14},{14... | collective-permute-start | bytes 786440 | tf_op jit(solution)/shard_map/ppermute | solution.py:604
  69.0 97.4 %collective-permute-start.4 = (bf16[2048,512]{1,0:T(8,128)(2,1)}, bf16[2048,512]{1,0:T(8,128)(2,1)}, u32[]{:S(2)}, u32[]{:S(2)}) collective-permute-start(bf16[2048,512]{1,0:T(8,128)(2,1)} %first_columns.1), channel_id=1, source_target_pairs={{0,1},{1,0},{2,3},{3,2},{4,5},{5,4},{6,7},{7,6},{8,9},{9,8},{10,11... | collective-permute-start | bytes 6291464 | tf_op jit(solution)/shard_map/ppermute | solution.py:553
  73.5 53.0 %copy-start.17 = (bf16[512,256]{1,0:T(8,128)(2,1)}, bf16[512,256]{1,0:T(8,128)(2,1)S(1)}, u32[]{:S(2)}) copy-start(bf16[512,256]{1,0:T(8,128)(2,1)S(1)} %inject.39.refs_7_.refs_6_.refs_5_.refs_4_) | copy-start | bytes 786436
  73.5 10.6 %collective-permute-start.11 = (bf16[512,256]{1,0:T(8,128)(2,1)S(1)}, bf16[512,256]{1,0:T(8,128)(2,1)S(1)}, u32[]{:S(2)}, u32[]{:S(2)}) collective-permute-start(bf16[512,256]{1,0:T(8,128)(2,1)S(1)} %inject.39.refs_7_.refs_6_.refs_5_.refs_4_), channel_id=1, source_target_pairs={{0,2},{2,6},{6,4},{4,0},{1,3},{3,7},{7,5},{5,1},{8,10},{10,14},{14... | collective-permute-start | bytes 786440 | tf_op jit(solution)/shard_map/ppermute | solution.py:604
  79.1 53.0 %copy-start.19 = (bf16[512,256]{1,0:T(8,128)(2,1)}, bf16[512,256]{1,0:T(8,128)(2,1)S(1)}, u32[]{:S(2)}) copy-start(bf16[512,256]{1,0:T(8,128)(2,1)S(1)} %inject.35.refs_2_.refs_1_.refs_0_) | copy-start | bytes 786436
  79.1 10.7 %collective-permute-start.7 = (bf16[512,256]{1,0:T(8,128)(2,1)S(1)}, bf16[512,256]{1,0:T(8,128)(2,1)S(1)}, u32[]{:S(2)}, u32[]{:S(2)}) collective-permute-start(bf16[512,256]{1,0:T(8,128)(2,1)S(1)} %inject.35.refs_2_.refs_1_.refs_0_), channel_id=1, source_target_pairs={{0,2},{2,6},{6,4},{4,0},{1,3},{3,7},{7,5},{5,1},{8,10},{10,14},{14... | collective-permute-start | bytes 786440 | tf_op jit(solution)/shard_map/ppermute | solution.py:604
  84.7 10.6 %collective-permute-start.12 = (bf16[512,256]{1,0:T(8,128)(2,1)S(1)}, bf16[512,256]{1,0:T(8,128)(2,1)S(1)}, u32[]{:S(2)}, u32[]{:S(2)}) collective-permute-start(bf16[512,256]{1,0:T(8,128)(2,1)S(1)} %inject.40.refs_8_.refs_7_.refs_6_.refs_5_.refs_4_), channel_id=1, source_target_pairs={{0,2},{2,6},{6,4},{4,0},{1,3},{3,7},{7,5},{5,1},{8,10},{10,14},{14... | collective-permute-start | bytes 786440 | tf_op jit(solution)/shard_map/ppermute | solution.py:604
  90.3 10.4 %collective-permute-start.8 = (bf16[512,256]{1,0:T(8,128)(2,1)S(1)}, bf16[512,256]{1,0:T(8,128)(2,1)S(1)}, u32[]{:S(2)}, u32[]{:S(2)}) collective-permute-start(bf16[512,256]{1,0:T(8,128)(2,1)S(1)} %inject.36.refs_3_.refs_2_.refs_1_.refs_0_), channel_id=1, source_target_pairs={{0,2},{2,6},{6,4},{4,0},{1,3},{3,7},{7,5},{5,1},{8,10},{10,14},{14... | collective-permute-start | bytes 786440 | tf_op jit(solution)/shard_map/ppermute | solution.py:604
  103.0 44.5 %collective-permute-start.13 = (bf16[2,2,512,256]{3,2,1,0:T(8,128)(2,1)}, bf16[2,2,512,256]{3,2,1,0:T(8,128)(2,1)}, u32[]{:S(2)}, u32[]{:S(2)}) collective-permute-start(bf16[2,2,512,256]{3,2,1,0:T(8,128)(2,1)} %gather_tiles.1), channel_id=1, source_target_pairs={{0,1},{1,0},{2,3},{3,2},{4,5},{5,4},{6,7},{7,6},{8,9},{9,8},{10,11... | collective-permute-start | bytes 3145736 | tf_op jit(solution)/shard_map/ppermute | solution.py:553
  104.5 10.1 %collective-permute-start.21 = (bf16[512,256]{1,0:T(8,128)(2,1)S(1)}, bf16[512,256]{1,0:T(8,128)(2,1)S(1)}, u32[]{:S(2)}, u32[]{:S(2)}) collective-permute-start(bf16[512,256]{1,0:T(8,128)(2,1)S(1)} %inject.41.refs_9_.refs_7_.refs_6_.refs_5_.refs_4_), channel_id=1, source_target_pairs={{0,2},{2,6},{6,4},{4,0},{1,3},{3,7},{7,5},{5,1},{8,10},{10,14},{14... | collective-permute-start | bytes 786440 | tf_op jit(solution)/shard_map/ppermute | solution.py:604
  105.3 15.0 %collective-permute-start.14 = (bf16[512,256]{1,0:T(8,128)(2,1)S(1)}, bf16[512,256]{1,0:T(8,128)(2,1)S(1)}, u32[]{:S(2)}, u32[]{:S(2)}) collective-permute-start(bf16[512,256]{1,0:T(8,128)(2,1)S(1)} %inject.37.refs_4_.refs_3_.refs_2_.refs_1_.refs_0_), channel_id=1, source_target_pairs={{0,2},{2,6},{6,4},{4,0},{1,3},{3,7},{7,5},{5,1},{8,10},{10,14},{14... | collective-permute-start | bytes 786440 | tf_op jit(solution)/shard_map/ppermute | solution.py:604
  115.3 21.9 %copy-start.15 = (bf16[512,256]{1,0:T(8,128)(2,1)}, bf16[512,256]{1,0:T(8,128)(2,1)S(1)}, u32[]{:S(2)}) copy-start(bf16[512,256]{1,0:T(8,128)(2,1)S(1)} %inject.48.refs_7_.refs_6_.refs_5_.refs_4_) | copy-start | bytes 786436
  115.3 10.6 %collective-permute-start.22 = (bf16[512,256]{1,0:T(8,128)(2,1)S(1)}, bf16[512,256]{1,0:T(8,128)(2,1)S(1)}, u32[]{:S(2)}, u32[]{:S(2)}) collective-permute-start(bf16[512,256]{1,0:T(8,128)(2,1)S(1)} %inject.48.refs_7_.refs_6_.refs_5_.refs_4_), channel_id=1, source_target_pairs={{0,2},{2,6},{6,4},{4,0},{1,3},{3,7},{7,5},{5,1},{8,10},{10,14},{14... | collective-permute-start | bytes 786440 | tf_op jit(solution)/shard_map/ppermute | solution.py:604
  120.8 10.7 %collective-permute-start.15 = (bf16[512,256]{1,0:T(8,128)(2,1)S(1)}, bf16[512,256]{1,0:T(8,128)(2,1)S(1)}, u32[]{:S(2)}, u32[]{:S(2)}) collective-permute-start(bf16[512,256]{1,0:T(8,128)(2,1)S(1)} %inject.42.refs_3_.refs_2_.refs_1_.refs_0_), channel_id=1, source_target_pairs={{0,2},{2,6},{6,4},{4,0},{1,3},{3,7},{7,5},{5,1},{8,10},{10,14},{14... | collective-permute-start | bytes 786440 | tf_op jit(solution)/shard_map/ppermute | solution.py:604
  126.5 10.6 %collective-permute-start.24 = (bf16[512,256]{1,0:T(8,128)(2,1)S(1)}, bf16[512,256]{1,0:T(8,128)(2,1)S(1)}, u32[]{:S(2)}, u32[]{:S(2)}) collective-permute-start(bf16[512,256]{1,0:T(8,128)(2,1)S(1)} %inject.49.refs_7_.refs_6_.refs_5_.refs_4_), channel_id=1, source_target_pairs={{0,2},{2,6},{6,4},{4,0},{1,3},{3,7},{7,5},{5,1},{8,10},{10,14},{14... | collective-permute-start | bytes 786440 | tf_op jit(solution)/shard_map/ppermute | solution.py:604
  132.1 9.8 %collective-permute-start.16 = (bf16[512,256]{1,0:T(8,128)(2,1)S(1)}, bf16[512,256]{1,0:T(8,128)(2,1)S(1)}, u32[]{:S(2)}, u32[]{:S(2)}) collective-permute-start(bf16[512,256]{1,0:T(8,128)(2,1)S(1)} %inject.43.refs_3_.refs_2_.refs_1_.refs_0_), channel_id=1, source_target_pairs={{0,2},{2,6},{6,4},{4,0},{1,3},{3,7},{7,5},{5,1},{8,10},{10,14},{14... | collective-permute-start | bytes 786440 | tf_op jit(solution)/shard_map/ppermute | solution.py:604
  132.9 32.8 %copy-start.3 = (bf16[16,512,256]{2,1,0:T(8,128)(2,1)S(1)}, bf16[16,512,256]{2,1,0:T(8,128)(2,1)}, u32[]{:S(2)}) copy-start(bf16[16,512,256]{2,1,0:T(8,128)(2,1)} %get-tuple-element.37.rows_ref) | copy-start | bytes 12582916
  137.1 2.2 copy-start.6
  139.9 37.3 %copy-start.11 = (bf16[512,256]{1,0:T(8,128)(2,1)}, bf16[512,256]{1,0:T(8,128)(2,1)S(1)}, u32[]{:S(2)}) copy-start(bf16[512,256]{1,0:T(8,128)(2,1)S(1)} %inject.51.refs_7_.refs_6_.refs_5_.refs_4_) | copy-start | bytes 786436
  139.9 21.0 %collective-permute-start.25 = (bf16[512,256]{1,0:T(8,128)(2,1)S(1)}, bf16[512,256]{1,0:T(8,128)(2,1)S(1)}, u32[]{:S(2)}, u32[]{:S(2)}) collective-permute-start(bf16[512,256]{1,0:T(8,128)(2,1)S(1)} %inject.51.refs_7_.refs_6_.refs_5_.refs_4_), channel_id=1, source_target_pairs={{0,2},{2,6},{6,4},{4,0},{1,3},{3,7},{7,5},{5,1},{8,10},{10,14},{14... | collective-permute-start | bytes 786440 | tf_op jit(solution)/shard_map/ppermute | solution.py:604
  141.8 2.2 copy-start.2
  144.6 32.7 %copy-start.13 = (bf16[512,256]{1,0:T(8,128)(2,1)}, bf16[512,256]{1,0:T(8,128)(2,1)S(1)}, u32[]{:S(2)}) copy-start(bf16[512,256]{1,0:T(8,128)(2,1)S(1)} %inject.44.refs_3_.refs_2_.refs_1_.refs_0_) | copy-start | bytes 786436
  144.6 21.1 %collective-permute-start.17 = (bf16[512,256]{1,0:T(8,128)(2,1)S(1)}, bf16[512,256]{1,0:T(8,128)(2,1)S(1)}, u32[]{:S(2)}, u32[]{:S(2)}) collective-permute-start(bf16[512,256]{1,0:T(8,128)(2,1)S(1)} %inject.44.refs_3_.refs_2_.refs_1_.refs_0_), channel_id=1, source_target_pairs={{0,2},{2,6},{6,4},{4,0},{1,3},{3,7},{7,5},{5,1},{8,10},{10,14},{14... | collective-permute-start | bytes 786440 | tf_op jit(solution)/shard_map/ppermute | solution.py:604
  161.0 2.2 copy-start.7
  163.8 29.9 %collective-permute-start.27 = (bf16[512,256]{1,0:T(8,128)(2,1)S(1)}, bf16[512,256]{1,0:T(8,128)(2,1)S(1)}, u32[]{:S(2)}, u32[]{:S(2)}) collective-permute-start(bf16[512,256]{1,0:T(8,128)(2,1)S(1)} %inject.52.refs_7_.refs_6_.refs_5_.refs_4_), channel_id=1, source_target_pairs={{0,2},{2,6},{6,4},{4,0},{1,3},{3,7},{7,5},{5,1},{8,10},{10,14},{14... | collective-permute-start | bytes 786440 | tf_op jit(solution)/shard_map/ppermute | solution.py:604
  166.3 12.3 %copy-start.9 = (bf16[512,256]{1,0:T(8,128)(2,1)}, bf16[512,256]{1,0:T(8,128)(2,1)S(1)}, u32[]{:S(2)}) copy-start(bf16[512,256]{1,0:T(8,128)(2,1)S(1)} %inject.45.refs_3_.refs_2_.refs_1_.refs_0_) | copy-start | bytes 786436
  166.3 10.9 %collective-permute-start.18 = (bf16[512,256]{1,0:T(8,128)(2,1)S(1)}, bf16[512,256]{1,0:T(8,128)(2,1)S(1)}, u32[]{:S(2)}, u32[]{:S(2)}) collective-permute-start(bf16[512,256]{1,0:T(8,128)(2,1)S(1)} %inject.45.refs_3_.refs_2_.refs_1_.refs_0_), channel_id=1, source_target_pairs={{0,2},{2,6},{6,4},{4,0},{1,3},{3,7},{7,5},{5,1},{8,10},{10,14},{14... | collective-permute-start | bytes 786440 | tf_op jit(solution)/shard_map/ppermute | solution.py:604
  177.8 25.6 %collective-permute-start.19 = (bf16[512,256]{1,0:T(8,128)(2,1)S(1)}, bf16[512,256]{1,0:T(8,128)(2,1)S(1)}, u32[]{:S(2)}, u32[]{:S(2)}) collective-permute-start(bf16[512,256]{1,0:T(8,128)(2,1)S(1)} %inject.46.refs_3_.refs_2_.refs_1_.refs_0_), channel_id=1, source_target_pairs={{0,2},{2,6},{6,4},{4,0},{1,3},{3,7},{7,5},{5,1},{8,10},{10,14},{14... | collective-permute-start | bytes 786440 | tf_op jit(solution)/shard_map/ppermute | solution.py:604
  186.8 6.9 %copy-start.8 = (bf16[16,512,256]{2,1,0:T(8,128)(2,1)S(1)}, bf16[16,512,256]{2,1,0:T(8,128)(2,1)}, u32[]{:S(2)}) copy-start(bf16[16,512,256]{2,1,0:T(8,128)(2,1)} %get-tuple-element.39.rows_ref) | copy-start | bytes 12582916
  186.8 9.9 %copy-start.21 = (bf16[512,256]{1,0:T(8,128)(2,1)S(1)}, bf16[512,256]{1,0:T(8,128)(2,1)}, u32[]{:S(2)}) copy-start(bf16[512,256]{1,0:T(8,128)(2,1)} %copy-done.19) | copy-start | bytes 786436
  194.3 11.7 %copy-start.16 = (bf16[512,256]{1,0:T(8,128)(2,1)S(1)}, bf16[512,256]{1,0:T(8,128)(2,1)}, u32[]{:S(2)}) copy-start(bf16[512,256]{1,0:T(8,128)(2,1)} %copy-done.15) | copy-start | bytes 786436
  194.3 18.0 %collective-permute-start.28 = (bf16[512,256]{1,0:T(8,128)(2,1)S(1)}, bf16[512,256]{1,0:T(8,128)(2,1)S(1)}, u32[]{:S(2)}, u32[]{:S(2)}) collective-permute-start(bf16[512,256]{1,0:T(8,128)(2,1)S(1)} %inject.54.refs_7_.refs_6_.refs_5_.refs_4_), channel_id=1, source_target_pairs={{0,2},{2,6},{6,4},{4,0},{1,3},{3,7},{7,5},{5,1},{8,10},{10,14},{14... | collective-permute-start | bytes 786440 | tf_op jit(solution)/shard_map/ppermute | solution.py:604
  204.0 15.5 %collective-permute-start.20 = (bf16[512,256]{1,0:T(8,128)(2,1)S(1)}, bf16[512,256]{1,0:T(8,128)(2,1)S(1)}, u32[]{:S(2)}, u32[]{:S(2)}) collective-permute-start(bf16[512,256]{1,0:T(8,128)(2,1)S(1)} %inject.47.refs_3_.refs_2_.refs_1_.refs_0_), channel_id=1, source_target_pairs={{0,2},{2,6},{6,4},{4,0},{1,3},{3,7},{7,5},{5,1},{8,10},{10,14},{14... | collective-permute-start | bytes 786440 | tf_op jit(solution)/shard_map/ppermute | solution.py:604
  213.0 7.9 %copy-start.12 = (bf16[512,256]{1,0:T(8,128)(2,1)S(1)}, bf16[512,256]{1,0:T(8,128)(2,1)}, u32[]{:S(2)}) copy-start(bf16[512,256]{1,0:T(8,128)(2,1)} %copy-done.11) | copy-start | bytes 786436
  213.0 7.9 %copy-start.14 = (bf16[512,256]{1,0:T(8,128)(2,1)S(1)}, bf16[512,256]{1,0:T(8,128)(2,1)}, u32[]{:S(2)}) copy-start(bf16[512,256]{1,0:T(8,128)(2,1)} %copy-done.13) | copy-start | bytes 786436
  213.0 14.3 %collective-permute-start.30 = (bf16[512,256]{1,0:T(8,128)(2,1)S(1)}, bf16[512,256]{1,0:T(8,128)(2,1)S(1)}, u32[]{:S(2)}, u32[]{:S(2)}) collective-permute-start(bf16[512,256]{1,0:T(8,128)(2,1)S(1)} %inject.55.refs_7_.refs_6_.refs_5_.refs_4_), channel_id=1, source_target_pairs={{0,2},{2,6},{6,4},{4,0},{1,3},{3,7},{7,5},{5,1},{8,10},{10,14},{14... | collective-permute-start | bytes 786440 | tf_op jit(solution)/shard_map/ppermute | solution.py:604
  220.1 10.2 %copy-start.10 = (bf16[512,256]{1,0:T(8,128)(2,1)S(1)}, bf16[512,256]{1,0:T(8,128)(2,1)}, u32[]{:S(2)}) copy-start(bf16[512,256]{1,0:T(8,128)(2,1)} %copy-done.9) | copy-start | bytes 786436
  220.1 16.6 %collective-permute-start.23 = (bf16[512,256]{1,0:T(8,128)(2,1)S(1)}, bf16[512,256]{1,0:T(8,128)(2,1)S(1)}, u32[]{:S(2)}, u32[]{:S(2)}) collective-permute-start(bf16[512,256]{1,0:T(8,128)(2,1)S(1)} %inject.50.refs_3_.refs_2_.refs_1_.refs_0_), channel_id=1, source_target_pairs={{0,2},{2,6},{6,4},{4,0},{1,3},{3,7},{7,5},{5,1},{8,10},{10,14},{14... | collective-permute-start | bytes 786440 | tf_op jit(solution)/shard_map/ppermute | solution.py:604
  227.9 17.9 %collective-permute-start.31 = (bf16[512,256]{1,0:T(8,128)(2,1)S(1)}, bf16[512,256]{1,0:T(8,128)(2,1)S(1)}, u32[]{:S(2)}, u32[]{:S(2)}) collective-permute-start(bf16[512,256]{1,0:T(8,128)(2,1)S(1)} %inject.57.refs_7_.refs_6_.refs_5_.refs_4_), channel_id=1, source_target_pairs={{0,2},{2,6},{6,4},{4,0},{1,3},{3,7},{7,5},{5,1},{8,10},{10,14},{14... | collective-permute-start | bytes 786440 | tf_op jit(solution)/shard_map/ppermute | solution.py:604
  237.2 15.6 %collective-permute-start.26 = (bf16[512,256]{1,0:T(8,128)(2,1)S(1)}, bf16[512,256]{1,0:T(8,128)(2,1)S(1)}, u32[]{:S(2)}, u32[]{:S(2)}) collective-permute-start(bf16[512,256]{1,0:T(8,128)(2,1)S(1)} %inject.53.refs_3_.refs_2_.refs_1_.refs_0_), channel_id=1, source_target_pairs={{0,2},{2,6},{6,4},{4,0},{1,3},{3,7},{7,5},{5,1},{8,10},{10,14},{14... | collective-permute-start | bytes 786440 | tf_op jit(solution)/shard_map/ppermute | solution.py:604
  246.4 14.2 %collective-permute-start.33 = (bf16[512,256]{1,0:T(8,128)(2,1)S(1)}, bf16[512,256]{1,0:T(8,128)(2,1)S(1)}, u32[]{:S(2)}, u32[]{:S(2)}) collective-permute-start(bf16[512,256]{1,0:T(8,128)(2,1)S(1)} %inject.58.refs_7_.refs_6_.refs_5_.refs_4_), channel_id=1, source_target_pairs={{0,2},{2,6},{6,4},{4,0},{1,3},{3,7},{7,5},{5,1},{8,10},{10,14},{14... | collective-permute-start | bytes 786440 | tf_op jit(solution)/shard_map/ppermute | solution.py:604
  253.5 16.6 %collective-permute-start.29 = (bf16[512,256]{1,0:T(8,128)(2,1)S(1)}, bf16[512,256]{1,0:T(8,128)(2,1)S(1)}, u32[]{:S(2)}, u32[]{:S(2)}) collective-permute-start(bf16[512,256]{1,0:T(8,128)(2,1)S(1)} %inject.56.refs_3_.refs_2_.refs_1_.refs_0_), channel_id=1, source_target_pairs={{0,2},{2,6},{6,4},{4,0},{1,3},{3,7},{7,5},{5,1},{8,10},{10,14},{14... | collective-permute-start | bytes 786440 | tf_op jit(solution)/shard_map/ppermute | solution.py:604
  261.2 17.7 %collective-permute-start.34 = (bf16[512,256]{1,0:T(8,128)(2,1)S(1)}, bf16[512,256]{1,0:T(8,128)(2,1)S(1)}, u32[]{:S(2)}, u32[]{:S(2)}) collective-permute-start(bf16[512,256]{1,0:T(8,128)(2,1)S(1)} %inject.60.refs_7_.refs_6_.refs_5_.refs_4_), channel_id=1, source_target_pairs={{0,2},{2,6},{6,4},{4,0},{1,3},{3,7},{7,5},{5,1},{8,10},{10,14},{14... | collective-permute-start | bytes 786440 | tf_op jit(solution)/shard_map/ppermute | solution.py:604
  270.6 15.7 %collective-permute-start.32 = (bf16[512,256]{1,0:T(8,128)(2,1)S(1)}, bf16[512,256]{1,0:T(8,128)(2,1)S(1)}, u32[]{:S(2)}, u32[]{:S(2)}) collective-permute-start(bf16[512,256]{1,0:T(8,128)(2,1)S(1)} %inject.59.refs_3_.refs_2_.refs_1_.refs_0_), channel_id=1, source_target_pairs={{0,2},{2,6},{6,4},{4,0},{1,3},{3,7},{7,5},{5,1},{8,10},{10,14},{14... | collective-permute-start | bytes 786440 | tf_op jit(solution)/shard_map/ppermute | solution.py:604
  279.5 10.1 %collective-permute-start.36 = (bf16[512,256]{1,0:T(8,128)(2,1)S(1)}, bf16[512,256]{1,0:T(8,128)(2,1)S(1)}, u32[]{:S(2)}, u32[]{:S(2)}) collective-permute-start(bf16[512,256]{1,0:T(8,128)(2,1)S(1)} %inject.61.refs_7_.refs_6_.refs_5_.refs_4_), channel_id=1, source_target_pairs={{0,2},{2,6},{6,4},{4,0},{1,3},{3,7},{7,5},{5,1},{8,10},{10,14},{14... | collective-permute-start | bytes 786440 | tf_op jit(solution)/shard_map/ppermute | solution.py:604
  286.9 10.1 %collective-permute-start.35 = (bf16[512,256]{1,0:T(8,128)(2,1)S(1)}, bf16[512,256]{1,0:T(8,128)(2,1)S(1)}, u32[]{:S(2)}, u32[]{:S(2)}) collective-permute-start(bf16[512,256]{1,0:T(8,128)(2,1)S(1)} %inject.62.refs_3_.refs_2_.refs_1_.refs_0_), channel_id=1, source_target_pairs={{0,2},{2,6},{6,4},{4,0},{1,3},{3,7},{7,5},{5,1},{8,10},{10,14},{14... | collective-permute-start | bytes 786440 | tf_op jit(solution)/shard_map/ppermute | solution.py:604
  290.2 12.0 %collective-permute-start.38 = (bf16[512,256]{1,0:T(8,128)(2,1)S(1)}, bf16[512,256]{1,0:T(8,128)(2,1)S(1)}, u32[]{:S(2)}, u32[]{:S(2)}) collective-permute-start(bf16[512,256]{1,0:T(8,128)(2,1)S(1)} %inject.63.refs_7_.refs_6_.refs_5_.refs_4_), channel_id=1, source_target_pairs={{0,2},{2,6},{6,4},{4,0},{1,3},{3,7},{7,5},{5,1},{8,10},{10,14},{14... | collective-permute-start | bytes 786440 | tf_op jit(solution)/shard_map/ppermute | solution.py:604
  297.6 11.7 %collective-permute-start.37 = (bf16[512,256]{1,0:T(8,128)(2,1)S(1)}, bf16[512,256]{1,0:T(8,128)(2,1)S(1)}, u32[]{:S(2)}, u32[]{:S(2)}) collective-permute-start(bf16[512,256]{1,0:T(8,128)(2,1)S(1)} %inject.64.refs_3_.refs_2_.refs_1_), channel_id=1, source_target_pairs={{0,2},{2,6},{6,4},{4,0},{1,3},{3,7},{7,5},{5,1},{8,10},{10,14},{14... | collective-permute-start | bytes 786440 | tf_op jit(solution)/shard_map/ppermute | solution.py:604
  302.8 10.7 %collective-permute-start.40 = (bf16[512,256]{1,0:T(8,128)(2,1)S(1)}, bf16[512,256]{1,0:T(8,128)(2,1)S(1)}, u32[]{:S(2)}, u32[]{:S(2)}) collective-permute-start(bf16[512,256]{1,0:T(8,128)(2,1)S(1)} %inject.65.refs_7_.refs_6_.refs_5_), channel_id=1, source_target_pairs={{0,2},{2,6},{6,4},{4,0},{1,3},{3,7},{7,5},{5,1},{8,10},{10,14},{14... | collective-permute-start | bytes 786440 | tf_op jit(solution)/shard_map/ppermute | solution.py:604
  309.9 11.3 %collective-permute-start.39 = (bf16[512,256]{1,0:T(8,128)(2,1)S(1)}, bf16[512,256]{1,0:T(8,128)(2,1)S(1)}, u32[]{:S(2)}, u32[]{:S(2)}) collective-permute-start(bf16[512,256]{1,0:T(8,128)(2,1)S(1)} %inject.66.refs_3_.refs_2_), channel_id=1, source_target_pairs={{0,2},{2,6},{6,4},{4,0},{1,3},{3,7},{7,5},{5,1},{8,10},{10,14},{14... | collective-permute-start | bytes 786440 | tf_op jit(solution)/shard_map/ppermute | solution.py:604
  314.1 7.3 %collective-permute-start.41 = (bf16[512,256]{1,0:T(8,128)(2,1)S(1)}, bf16[512,256]{1,0:T(8,128)(2,1)S(1)}, u32[]{:S(2)}, u32[]{:S(2)}) collective-permute-start(bf16[512,256]{1,0:T(8,128)(2,1)S(1)} %inject.67.refs_7_.refs_6_), channel_id=1, source_target_pairs={{0,2},{2,6},{6,4},{4,0},{1,3},{3,7},{7,5},{5,1},{8,10},{10,14},{14... | collective-permute-start | bytes 786440 | tf_op jit(solution)/shard_map/ppermute | solution.py:604
  (16 other events, 18.0 us)
